TPU v7x, 256 devices: a whole 4x4x8 slice. The times are simulated.
256 devices in a mesh: slab: 64 (over z, x, core), tile: 4 (over y).
Axes of the slice: x: 4, y: 4, z: 8, core: 2. Of those that a mesh axis runs over, the one named last changes fastest.
Arguments:
- volume: float32 [1024, 256, 512], P('slab', 'tile'), may hold values from -6 to 6
- knot_bins: int32 [8], replicated, may hold values from 0 to 255, as said below
- colour_table: float32 [4, 8], replicated, may hold values from 0.001 to 1
- view_side: int32 [512], replicated, may hold values from 0 to 1
Outputs:
- image: float32 [4, 64, 4, 512], P(None, 'slab', 'tile')
Inputs may be any that keep to these rules, and one draw needn't show every extreme that they name: `knot_bins`: strictly increasing; the first is 0 and the last is 255.
All inputs are finite; a program needn't handle non-finite values.
Results may differ from a plain program's by a relative error of at most 0.0003.
Values sent between devices are 32-bit elements; how exact they have to be, the bound alone decides.
No kernel may reach another device: no remote copies, remote signals or barrier semaphores. Data moves between devices by JAX's collectives and lax.ppermute only.
A program may use at most 64 MiB of HBM per device.

v0:
```python
import jax
import jax.numpy as jnp
from jax import lax
from jax.sharding import PartitionSpec as P

BINS = 256


def with_halo(x, sides, width):
    for axis, dim in sides:
        size, length = (lax.axis_size(axis), x.shape[dim])
        up = [(i, (i + 1) % size) for i in range(size - 1)]
        down = [(j, i) for i, j in up]
        last = lax.slice_in_dim(x, length - width, length, axis=dim)
        leading = lax.slice_in_dim(x, 0, width, axis=dim)
        before = lax.ppermute(last, axis, up)
        after = lax.ppermute(leading, axis, down)
        x = jnp.concatenate([before, x, after], axis=dim)
    return x


def partner_2(block, axis, distance):
    count = lax.axis_size(axis)
    route = []
    for low in range(count):
        high = low | 1 << distance
        if high != low and high < count:
            route += [(low, high), (high, low)]
    return lax.ppermute(block, axis, route)


def axis_diff(values, axis):
    count = values.shape[axis]
    edge = jnp.zeros_like(lax.slice_in_dim(values, 0, 1, axis=axis))
    upper = jnp.concatenate([lax.slice_in_dim(values, 1, count, axis=axis), edge], axis=axis)
    lower_part = jnp.concatenate(
        [edge, lax.slice_in_dim(values, 0, count - 1, axis=axis)], axis=axis
    )
    return (upper - lower_part) * 0.5


def sample_terms(
    centre, deriv_depth, deriv_rows, deriv_cols, knot_bins, colour_table, total_planes
):
    sample = jnp.clip((centre + 3.0) / 6.0, 0.0, 1.0) * (BINS - 1)
    knot_pos = knot_bins.astype(jnp.float32)
    last = knot_bins.shape[0] - 2
    totals = [jnp.zeros_like(sample) for channel in range(4)]
    for knot in range(last + 1):
        lower_edge = knot_pos[knot]
        upper_edge = knot_pos[knot + 1]
        fraction = (sample - lower_edge) / (upper_edge - lower_edge)
        if knot == last:
            inside = (sample >= lower_edge) & (sample <= upper_edge)
        else:
            inside = (sample >= lower_edge) & (sample < upper_edge)
        for channel in range(4):
            start_value = colour_table[channel, knot]
            rising = colour_table[channel, knot + 1] - start_value
            totals[channel] = totals[channel] + jnp.where(
                inside, start_value + fraction * rising, 0.0
            )
    length = jnp.sqrt(
        deriv_depth * deriv_depth + deriv_rows * deriv_rows + deriv_cols * deriv_cols + 1.0
    )
    shading = (
        0.3 + 0.7 * jnp.abs(0.64 * deriv_depth + 0.6 * deriv_rows + 0.48 * deriv_cols) / length
    )
    passed = jnp.exp(-totals[3] * (400.0 / total_planes))
    emitted = jnp.stack([(1.0 - passed) * totals[channel] * shading for channel in range(3)])
    return (passed, emitted)


def merge_pair(mine, partner, mine_front):
    front = jnp.where(mine_front, mine, partner)
    behind = jnp.where(mine_front, partner, mine)
    colour = front[:3] + front[3:4] * behind[:3]
    passing = front[3:4] * behind[3:4]
    return jnp.concatenate([colour, passing], axis=0)


def per_device(volume, knot_bins, colour_table, view_side):
    planes, tile_rows, columns = volume.shape
    slab_count = lax.axis_size("slab")
    block_rows = tile_rows // slab_count
    padded = with_halo(volume, (("slab", 0), ("tile", 1)), 1)
    centre = padded[1:-1, 1:-1]
    deriv_depth = (padded[2:, 1:-1] - padded[:-2, 1:-1]) * 0.5
    deriv_rows = (padded[1:-1, 2:] - padded[1:-1, :-2]) * 0.5
    deriv_cols = axis_diff(centre, 2)
    passed, emitted = sample_terms(
        centre, deriv_depth, deriv_rows, deriv_cols, knot_bins, colour_table, planes * slab_count
    )
    toward = view_side == 1
    forward_prod = jnp.cumprod(passed, axis=0)
    backward_prod = jnp.flip(jnp.cumprod(jnp.flip(passed, 0), axis=0), 0)
    single = jnp.ones((1, tile_rows, columns), jnp.float32)
    ahead = jnp.concatenate([single, forward_prod[:-1]], axis=0)
    behind = jnp.concatenate([backward_prod[1:], single], axis=0)
    weight = jnp.where(toward, ahead, behind)
    colour = jnp.sum(weight[None] * emitted, axis=1)
    partial_value = jnp.concatenate([colour, forward_prod[-1][None]], axis=0)
    slab_index = lax.axis_index("slab")
    rounds = slab_count.bit_length() - 1
    current = partial_value
    for level in range(rounds):
        remaining = slab_count >> level
        shaped = current.reshape(4, remaining // 2, 2, block_rows, columns)
        upper_half = slab_index >> level & 1
        lower_group = upper_half == 0
        kept_half = jnp.where(lower_group, shaped[:, :, 0], shaped[:, :, 1])
        sent_half = jnp.where(lower_group, shaped[:, :, 1], shaped[:, :, 0])
        partner = partner_2(sent_half, "slab", level)
        mine_front = toward == lower_group
        current = merge_pair(kept_half, partner, mine_front).reshape(
            4, remaining // 2 * block_rows, columns
        )
    result = jnp.concatenate([current[:3], 1.0 - current[3:4]], axis=0)
    return result[:, None]


def solution(mesh):
    return jax.shard_map(
        per_device,
        mesh=mesh,
        in_specs=(P("slab", "tile", None), P(), P(), P()),
        out_specs=P(None, "slab", "tile", None),
        check_vma=False,
    )
```

profile of v0, /device:TPU:8, one launch (start us, length us, event | category | flops | bytes accessed | tf_op | source)
XLA Modules:
  0.0 181.3 jit_solution(2432570822194704783)
XLA Ops:
  0.0 1.0 fusion.21
  1.0 1.7 collective-permute-start.1
  2.7 1.3 collective-permute-start
  4.1 5.1 %fusion.22 = (f32[16,64,511]{2,1,0:T(8,128)}, f32[16,64,511]{2,1,0:T(8,128)}) fusion(f32[16,64,512]{2,1,0:T(8,128)} %param.4), kind=kLoop, calls=%fused_computation.107 | loop fusion | bytes 8372224 | tf_op jit(solution)/shard_map/slice | solution.py:35
  9.9 0.7 fusion.30
  10.9 1.4 copy-done.6
  12.4 3.5 %collective-permute-start.3 = (f32[18,1,512]{2,1,0:T(1,128)S(1)}, f32[18,1,512]{2,1,0:T(1,128)S(1)}, u32[]{:S(2)}, u32[]{:S(2)}) collective-permute-start(f32[18,1,512]{2,1,0:T(1,128)S(1)} %get-tuple-element.11), channel_id=1, source_target_pairs={{0,1},{1,2},{2,3},{4,5},{5,6},{6,7},{8,9},{9,10},{10,11},{12,13},{... | collective-permute-start | bytes 110600 | tf_op jit(solution)/shard_map/ppermute | solution.py:16
  15.9 2.4 %collective-permute-start.2 = (f32[18,1,512]{2,1,0:T(1,128)S(1)}, f32[18,1,512]{2,1,0:T(1,128)S(1)}, u32[]{:S(2)}, u32[]{:S(2)}) collective-permute-start(f32[18,1,512]{2,1,0:T(1,128)S(1)} %get-tuple-element.10), channel_id=1, source_target_pairs={{1,0},{2,1},{3,2},{5,4},{6,5},{7,6},{9,8},{10,9},{11,10},{13,12},{... | collective-permute-start | bytes 110600 | tf_op jit(solution)/shard_map/ppermute | solution.py:17
  63.0 26.6 %multiply_bitcast_fusion.2 = (f32[1,16,64,512]{3,2,1,0:T(8,128)}, f32[16,64,512]{2,1,0:T(8,128)}, f32[16,64,512]{2,1,0:T(8,128)S(1)}) fusion(f32[]{:T(128)S(6)} %sub.192, f32[]{:T(128)} %bitcast.22, f32[]{:T(128)S(6)} %sub.191, f32[]{:T(128)} %bitcast.21, f32[]{:T(128)S(6)} %sub.190, f32[]{:T(128)} %bitcast.20, f32[]{:T(128)S(6)} %sub.189, f32[]{:T(128)} %bitcast.19, ...), kind=kLoop, calls=%fused_computation.10 | loop fusion | flops 64487424 | bytes 15270060 | tf_op jit(solution)/shard_map/stack | solution.py:70
  89.6 1.4 copy-done.1
  91.0 1.5 fusion.33
  92.5 3.2 %rev.5 = f32[16,64,512]{2,1,0:T(8,128)} reverse(f32[16,64,512]{2,1,0:T(8,128)} %copy-done.1), dimensions={0} | reverse | bytes 4194304 | tf_op jit(solution)/shard_map/jit(_flip)/rev | solution.py:96
  95.7 3.2 %slice.419 = f32[15,64,512]{2,1,0:T(8,128)} slice(f32[16,64,512]{2,1,0:T(8,128)} %fusion.33), slice={[0:15], [0:64], [0:512]} | slice | bytes 3932160 | tf_op jit(solution)/shard_map/slice | solution.py:98
  98.9 5.8 %fusion.34 = f32[16,64,512]{2,1,0:T(8,128)S(1)} fusion(f32[16,64,512]{2,1,0:T(8,128)S(1)} %copy-done.4), kind=kOutput, calls=%fused_computation.119 | output fusion | flops 7864320 | bytes 4194304 | tf_op jit(solution)/shard_map/jit(cumprod)/reduce_window | solution.py:96
  104.7 1.4 slice.420
  106.2 3.1 %slice.346 = f32[15,64,512]{2,1,0:T(8,128)} reverse(f32[15,64,512]{2,1,0:T(8,128)} %slice.420), dimensions={0} | reverse | bytes 3932160 | tf_op jit(solution)/shard_map/slice | solution.py:99
  109.3 2.7 %pad_select_fusion = f32[16,64,512]{2,1,0:T(8,128)S(1)} fusion(f32[15,64,512]{2,1,0:T(8,128)} %slice.346, f32[15,64,512]{2,1,0:T(8,128)} %slice.419, pred[512]{0:T(512)(128)(4,1)S(1)} %get-tuple-element.6), kind=kLoop, calls=%fused_computation.12 | loop fusion | flops 524288 | bytes 6029824 | tf_op jit(solution)/shard_map/jit(_where)/select_n | solution.py:100
  112.7 14.2 %multiply_bitcast_fusion = f32[1,16,64,512]{3,2,1,0:T(8,128)S(1)} fusion(f32[16,64,512]{2,1,0:T(8,128)S(1)} %copy-done.3, f32[16,64,512]{2,1,0:T(8,128)S(1)} %copy-done.2, f32[]{:T(128)S(6)} %sub.209, f32[]{:T(128)} %bitcast.40, f32[]{:T(128)S(6)} %sub.208, f32[]{:T(128)} %bitcast.39, f32[]{:T(128)S(6)} %sub.207, f32[]{:T(128)} %bitcast.38, f32[]{:T(128)S(6)} %sub.206, ...), kind=kLoop, calls=%fused_computation.8 | loop fusion | flops 36175872 | bytes 8388724 | tf_op jit(solution)/shard_map/stack | solution.py:70
  126.9 14.3 %multiply_bitcast_fusion.1 = f32[1,16,64,512]{3,2,1,0:T(8,128)S(1)} fusion(f32[16,64,512]{2,1,0:T(8,128)S(1)} %copy-done.3, f32[16,64,512]{2,1,0:T(8,128)S(1)} %copy-done.2, f32[]{:T(128)S(6)} %sub.202, f32[]{:T(128)} %bitcast.31, f32[]{:T(128)S(6)} %sub.201, f32[]{:T(128)} %bitcast.30, f32[]{:T(128)S(6)} %sub.200, f32[]{:T(128)} %bitcast.29, f32[]{:T(128)S(6)} %sub.199, ...), kind=kLoop, calls=%fused_computation.9 | loop fusion | flops 36175872 | bytes 8388724 | tf_op jit(solution)/shard_map/stack | solution.py:70
  141.2 1.1 fusion
  142.7 1.9 %collective-permute-start.4 = (f32[4,32,1,512]{3,0,1,2:T(4,128)S(1)}, f32[4,32,1,512]{3,0,1,2:T(4,128)S(1)}, u32[]{:S(2)}, u32[]{:S(2)}) collective-permute-start(f32[4,32,1,512]{3,0,1,2:T(4,128)S(1)} %select_bitcast_fusion), channel_id=1, source_target_pairs={{0,4},{4,0},{8,12},{12,8},{16,20},{20,16},{24,28},{28,24},{32,36},... | collective-permute-start | bytes 786440 | tf_op jit(solution)/shard_map/ppermute | solution.py:29
  144.7 1.2 collective-permute-done.4
  146.4 2.6 %collective-permute-start.5 = (f32[4,16,1,512]{3,0,1,2:T(4,128)S(1)}, f32[4,16,1,512]{3,0,1,2:T(4,128)S(1)}, u32[]{:S(2)}, u32[]{:S(2)}) collective-permute-start(f32[4,16,1,512]{3,0,1,2:T(4,128)S(1)} %select_bitcast_fusion.1), channel_id=1, source_target_pairs={{0,8},{8,0},{4,12},{12,4},{16,24},{24,16},{20,28},{28,20},{32,40},... | collective-permute-start | bytes 393224 | tf_op jit(solution)/shard_map/ppermute | solution.py:29
  149.0 3.8 %collective-permute-done.5 = f32[4,16,1,512]{3,0,1,2:T(4,128)S(1)} collective-permute-done((f32[4,16,1,512]{3,0,1,2:T(4,128)S(1)}, f32[4,16,1,512]{3,0,1,2:T(4,128)S(1)}, u32[]{:S(2)}, u32[]{:S(2)}) %collective-permute-start.5) | collective-permute-done | bytes 131104 | tf_op jit(solution)/shard_map/ppermute | solution.py:29
  153.1 3.4 %collective-permute-start.6 = (f32[4,8,1,512]{3,0,1,2:T(4,128)S(1)}, f32[4,8,1,512]{3,0,1,2:T(4,128)S(1)}, u32[]{:S(2)}, u32[]{:S(2)}) collective-permute-start(f32[4,8,1,512]{3,0,1,2:T(4,128)S(1)} %select_bitcast_fusion.2), channel_id=1, source_target_pairs={{0,16},{16,0},{4,20},{20,4},{8,24},{24,8},{12,28},{28,12},{32,48},... | collective-permute-start | bytes 196616 | tf_op jit(solution)/shard_map/ppermute | solution.py:29
  156.5 2.5 %collective-permute-done.6 = f32[4,8,1,512]{3,0,1,2:T(4,128)S(1)} collective-permute-done((f32[4,8,1,512]{3,0,1,2:T(4,128)S(1)}, f32[4,8,1,512]{3,0,1,2:T(4,128)S(1)}, u32[]{:S(2)}, u32[]{:S(2)}) %collective-permute-start.6) | collective-permute-done | bytes 65568 | tf_op jit(solution)/shard_map/ppermute | solution.py:29
  159.2 4.4 %collective-permute-start.7 = (f32[4,4,1,512]{3,0,1,2:T(4,128)S(1)}, f32[4,4,1,512]{3,0,1,2:T(4,128)S(1)}, u32[]{:S(2)}, u32[]{:S(2)}) collective-permute-start(f32[4,4,1,512]{3,0,1,2:T(4,128)S(1)} %select_bitcast_fusion.3), channel_id=1, source_target_pairs={{0,32},{32,0},{4,36},{36,4},{8,40},{40,8},{12,44},{44,12},{16,48},... | collective-permute-start | bytes 98312 | tf_op jit(solution)/shard_map/ppermute | solution.py:29
  163.5 1.9 %collective-permute-done.7 = f32[4,4,1,512]{3,0,1,2:T(4,128)S(1)} collective-permute-done((f32[4,4,1,512]{3,0,1,2:T(4,128)S(1)}, f32[4,4,1,512]{3,0,1,2:T(4,128)S(1)}, u32[]{:S(2)}, u32[]{:S(2)}) %collective-permute-start.7) | collective-permute-done | bytes 32800 | tf_op jit(solution)/shard_map/ppermute | solution.py:29
  165.6 3.5 %collective-permute-start.8 = (f32[4,2,1,512]{3,2,1,0:T(1,128)S(1)}, f32[4,2,1,512]{3,2,1,0:T(1,128)S(1)}, u32[]{:S(2)}, u32[]{:S(2)}) collective-permute-start(f32[4,2,1,512]{3,2,1,0:T(1,128)S(1)} %fusion.12), channel_id=1, source_target_pairs={{0,64},{64,0},{4,68},{68,4},{8,72},{72,8},{12,76},{76,12},{16,80},... | collective-permute-start | bytes 49160 | tf_op jit(solution)/shard_map/ppermute | solution.py:29
  169.0 1.7 collective-permute-done.8
  170.9 8.1 %collective-permute-start.9 = (f32[4,1,1,512]{3,1,2,0:T(1,128)S(1)}, f32[4,1,1,512]{3,1,2,0:T(1,128)S(1)}, u32[]{:S(2)}, u32[]{:S(2)}) collective-permute-start(f32[4,1,1,512]{3,1,2,0:T(1,128)S(1)} %fusion.15), channel_id=1, source_target_pairs={{0,128},{128,0},{4,132},{132,4},{8,136},{136,8},{12,140},{140,12},... | collective-permute-start | bytes 24584 | tf_op jit(solution)/shard_map/ppermute | solution.py:29
  179.0 1.6 collective-permute-done.9
  (71 shorter events, 4.6 us)
Async XLA Ops:
  1.0 9.7 %collective-permute-start.1 = (f32[1,64,512]{2,1,0:T(8,128)S(1)}, f32[1,64,512]{2,1,0:T(8,128)S(1)}, u32[]{:S(2)}, u32[]{:S(2)}) collective-permute-start(f32[1,64,512]{2,1,0:T(8,128)S(1)} %get-tuple-element.13), channel_id=1, source_target_pairs={{0,4},{4,8},{8,12},{12,16},{16,20},{20,24},{24,28},{28,32},{32,36}... | collective-permute-start | bytes 393224 | tf_op jit(solution)/shard_map/ppermute | solution.py:16
  2.7 8.2 %collective-permute-start = (f32[1,64,512]{2,1,0:T(8,128)S(1)}, f32[1,64,512]{2,1,0:T(8,128)S(1)}, u32[]{:S(2)}, u32[]{:S(2)}) collective-permute-start(f32[1,64,512]{2,1,0:T(8,128)S(1)} %get-tuple-element.12), channel_id=1, source_target_pairs={{4,0},{8,4},{12,8},{16,12},{20,16},{24,20},{28,24},{32,28},{36,32}... | collective-permute-start | bytes 393224 | tf_op jit(solution)/shard_map/ppermute | solution.py:17
  4.0 5.1 %copy-start.8 = (s32[512]{0:T(512)S(1)}, s32[512]{0:T(512)}, u32[]{:S(2)}) copy-start(s32[512]{0:T(512)} %param.7) | copy-start | bytes 6148
  4.1 5.1 %copy-start.7 = (f32[4,8]{1,0:T(4,128)S(1)}, f32[4,8]{1,0:T(4,128)}, u32[]{:S(2)}) copy-start(f32[4,8]{1,0:T(4,128)} %param.6) | copy-start | bytes 388
  4.1 5.8 %copy-start.9 = (s32[8]{0:T(128)S(1)}, s32[8]{0:T(128)}, u32[]{:S(2)}) copy-start(s32[8]{0:T(128)} %param.5) | copy-start | bytes 100
  4.1 6.6 %copy-start = (f32[16,64,512]{2,1,0:T(8,128)S(1)}, f32[16,64,512]{2,1,0:T(8,128)}, u32[]{:S(2)}) copy-start(f32[16,64,512]{2,1,0:T(8,128)} %param.4) | copy-start | bytes 6291460
  10.9 1.4 copy-start.6
  12.4 50.6 %collective-permute-start.3 = (f32[18,1,512]{2,1,0:T(1,128)S(1)}, f32[18,1,512]{2,1,0:T(1,128)S(1)}, u32[]{:S(2)}, u32[]{:S(2)}) collective-permute-start(f32[18,1,512]{2,1,0:T(1,128)S(1)} %get-tuple-element.11), channel_id=1, source_target_pairs={{0,1},{1,2},{2,3},{4,5},{5,6},{6,7},{8,9},{9,10},{10,11},{12,13},{... | collective-permute-start | bytes 110600 | tf_op jit(solution)/shard_map/ppermute | solution.py:16
  15.9 47.1 %collective-permute-start.2 = (f32[18,1,512]{2,1,0:T(1,128)S(1)}, f32[18,1,512]{2,1,0:T(1,128)S(1)}, u32[]{:S(2)}, u32[]{:S(2)}) collective-permute-start(f32[18,1,512]{2,1,0:T(1,128)S(1)} %get-tuple-element.10), channel_id=1, source_target_pairs={{1,0},{2,1},{3,2},{5,4},{6,5},{7,6},{9,8},{10,9},{11,10},{13,12},{... | collective-permute-start | bytes 110600 | tf_op jit(solution)/shard_map/ppermute | solution.py:17
  89.6 1.4 copy-start.1
  95.7 3.3 %copy-start.4 = (f32[16,64,512]{2,1,0:T(8,128)S(1)}, f32[16,64,512]{2,1,0:T(8,128)}, u32[]{:S(2)}) copy-start(f32[16,64,512]{2,1,0:T(8,128)} %rev.5) | copy-start | bytes 6291460
  109.3 2.8 %copy-start.2 = (f32[16,64,512]{2,1,0:T(8,128)S(1)}, f32[16,64,512]{2,1,0:T(8,128)}, u32[]{:S(2)}) copy-start(f32[16,64,512]{2,1,0:T(8,128)} %copy-done.1) | copy-start | bytes 6291460
  109.3 3.4 %copy-start.3 = (f32[16,64,512]{2,1,0:T(8,128)S(1)}, f32[16,64,512]{2,1,0:T(8,128)}, u32[]{:S(2)}) copy-start(f32[16,64,512]{2,1,0:T(8,128)} %get-tuple-element.8) | copy-start | bytes 6291460
  126.9 14.3 %copy-start.5 = (f32[1,16,64,512]{3,2,1,0:T(8,128)S(1)}, f32[1,16,64,512]{3,2,1,0:T(8,128)}, u32[]{:S(2)}) copy-start(f32[1,16,64,512]{3,2,1,0:T(8,128)} %get-tuple-element.7) | copy-start | bytes 6291460
  141.1 1.1 slice-start
  142.7 3.1 %collective-permute-start.4 = (f32[4,32,1,512]{3,0,1,2:T(4,128)S(1)}, f32[4,32,1,512]{3,0,1,2:T(4,128)S(1)}, u32[]{:S(2)}, u32[]{:S(2)}) collective-permute-start(f32[4,32,1,512]{3,0,1,2:T(4,128)S(1)} %select_bitcast_fusion), channel_id=1, source_target_pairs={{0,4},{4,0},{8,12},{12,8},{16,20},{20,16},{24,28},{28,24},{32,36},... | collective-permute-start | bytes 786440 | tf_op jit(solution)/shard_map/ppermute | solution.py:29
  146.4 6.4 %collective-permute-start.5 = (f32[4,16,1,512]{3,0,1,2:T(4,128)S(1)}, f32[4,16,1,512]{3,0,1,2:T(4,128)S(1)}, u32[]{:S(2)}, u32[]{:S(2)}) collective-permute-start(f32[4,16,1,512]{3,0,1,2:T(4,128)S(1)} %select_bitcast_fusion.1), channel_id=1, source_target_pairs={{0,8},{8,0},{4,12},{12,4},{16,24},{24,16},{20,28},{28,20},{32,40},... | collective-permute-start | bytes 393224 | tf_op jit(solution)/shard_map/ppermute | solution.py:29
  153.1 5.9 %collective-permute-start.6 = (f32[4,8,1,512]{3,0,1,2:T(4,128)S(1)}, f32[4,8,1,512]{3,0,1,2:T(4,128)S(1)}, u32[]{:S(2)}, u32[]{:S(2)}) collective-permute-start(f32[4,8,1,512]{3,0,1,2:T(4,128)S(1)} %select_bitcast_fusion.2), channel_id=1, source_target_pairs={{0,16},{16,0},{4,20},{20,4},{8,24},{24,8},{12,28},{28,12},{32,48},... | collective-permute-start | bytes 196616 | tf_op jit(solution)/shard_map/ppermute | solution.py:29
  159.2 6.3 %collective-permute-start.7 = (f32[4,4,1,512]{3,0,1,2:T(4,128)S(1)}, f32[4,4,1,512]{3,0,1,2:T(4,128)S(1)}, u32[]{:S(2)}, u32[]{:S(2)}) collective-permute-start(f32[4,4,1,512]{3,0,1,2:T(4,128)S(1)} %select_bitcast_fusion.3), channel_id=1, source_target_pairs={{0,32},{32,0},{4,36},{36,4},{8,40},{40,8},{12,44},{44,12},{16,48},... | collective-permute-start | bytes 98312 | tf_op jit(solution)/shard_map/ppermute | solution.py:29
  165.6 5.2 %collective-permute-start.8 = (f32[4,2,1,512]{3,2,1,0:T(1,128)S(1)}, f32[4,2,1,512]{3,2,1,0:T(1,128)S(1)}, u32[]{:S(2)}, u32[]{:S(2)}) collective-permute-start(f32[4,2,1,512]{3,2,1,0:T(1,128)S(1)} %fusion.12), channel_id=1, source_target_pairs={{0,64},{64,0},{4,68},{68,4},{8,72},{72,8},{12,76},{76,12},{16,80},... | collective-permute-start | bytes 49160 | tf_op jit(solution)/shard_map/ppermute | solution.py:29
  170.9 9.8 %collective-permute-start.9 = (f32[4,1,1,512]{3,1,2,0:T(1,128)S(1)}, f32[4,1,1,512]{3,1,2,0:T(1,128)S(1)}, u32[]{:S(2)}, u32[]{:S(2)}) collective-permute-start(f32[4,1,1,512]{3,1,2,0:T(1,128)S(1)} %fusion.15), channel_id=1, source_target_pairs={{0,128},{128,0},{4,132},{132,4},{8,136},{136,8},{12,140},{140,12},... | collective-permute-start | bytes 24584 | tf_op jit(solution)/shard_map/ppermute | solution.py:29
where the time goes:
time: 183 us; the launch traced here: 181 us
  other arithmetic  68 us (37%)
  between operations  44.6 us (24%)
  starting transfers between devices  32.8 us (18%)
  local copies, waits for them, and re-layouts  23.3 us (13%)
  waiting for transfers between devices  12.7 us (7%)
    another operation x3, other arithmetic, sample_terms(): jnp.stack([(1.0 - passed) * totals[channel] * shading for channel in rang...  55 us
    ppermute x6, starting transfers between devices, partner_2(): return lax.ppermute(block, axis, route)  23.9 us
    ppermute x6, waiting for transfers between devices, partner_2(): return lax.ppermute(block, axis, route)  12.7 us
    another operation x1, other arithmetic, per_device(): backward_prod = jnp.flip(jnp.cumprod(jnp.flip(passed, 0), axis=0), 0)  5.79 us
    ppermute x2, starting transfers between devices, with_halo(): before = lax.ppermute(last, axis, up)  5.23 us
    slice x1, local copies, waits for them, and re-layouts, axis_diff(): lax.slice_in_dim(values, 1, count, axis=axis)  5.08 us
    slice x2, local copies, waits for them, and re-layouts, per_device(): behind = jnp.concatenate([backward_prod[1:], single], axis=0)  4.58 us
    unnamed x27, local copies, waits for them, and re-layouts  3.69 us
  transfers between devices with their start and end apart: 10, of which 6 were waited for; matrix products, arithmetic and copies ran while one was open for 4% of the time, Pallas kernels for 0%

commit v1 on v0

v1 whole, which is shorter than its diff:
```python
import jax
import jax.numpy as jnp
from jax import lax
from jax.experimental import pallas as pl
from jax.experimental.pallas import tpu as pltpu
from jax.sharding import PartitionSpec as P

BINS = 256
KNOTS = 8
LOG2_E = 1.4426950408889634
LANES = 128
ROWS = 8


def knot_tables(knot_bins, colour_table, total_planes):
    sublane = lax.broadcasted_iota(jnp.int32, (ROWS, LANES), 0)

    def spread(read):
        table = jnp.full((ROWS, LANES), read(0), jnp.float32)
        for knot in range(1, KNOTS):
            table = jnp.where(sublane == knot, read(knot), table)
        return table

    def position(knot):
        return knot_bins[knot].astype(jnp.float32)

    scale = 6.0 / (BINS - 1)
    knot_at = spread(position) * scale - 3.0
    knot_at = jnp.where(sublane == KNOTS - 1, 3.0, knot_at)
    width = pltpu.roll(knot_at, KNOTS - 1, 0) - knot_at
    starts, slopes = [], []
    for channel in range(4):
        start = spread(lambda knot: colour_table[channel, knot])
        rise = (pltpu.roll(start, KNOTS - 1, 0) - start) / width
        slope = jnp.where(sublane == KNOTS - 1, 0.0, rise)
        factor = -400.0 / total_planes * LOG2_E if channel == 3 else 1.0
        starts.append(start * factor)
        slopes.append(slope * factor)
    edges = [jnp.broadcast_to(knot_at[k : k + 1], (ROWS, LANES)) for k in range(KNOTS)]
    return knot_at, edges, starts, slopes


def look_up(value, tables):
    knot_at, edges, starts, slopes = tables
    index = jnp.zeros(value.shape, jnp.int32)
    for knot in range(1, KNOTS):
        index = jnp.where(value >= edges[knot], knot, index)

    def pick(table):
        return jnp.take_along_axis(table, index, axis=0, mode="promise_in_bounds")

    offset = value - pick(knot_at)
    return [pick(starts[c]) + offset * pick(slopes[c]) for c in range(4)]


def march_kernel(
    total_planes, core_ref, knot_ref, colour_ref, volume, above, below, row_prev, row_next, side_ref,
    send_ref, keep_ref, pad, stage, sems,
):
    planes, tile_rows, columns = volume.shape
    blocks = tile_rows // ROWS
    pieces = columns // LANES

    def fetch(block):
        rows = pl.ds(pl.multiple_of(block * ROWS, ROWS), ROWS)
        padded = pl.ds(pl.multiple_of(block * ROWS + ROWS, ROWS), ROWS)
        return pltpu.make_async_copy(volume.at[:, rows], pad.at[:, padded], sems.at[block])

    for block in range(blocks):
        fetch(block).start()
    for plane in range(planes):
        pad[plane, ROWS - 1 : ROWS, :] = row_prev[plane]
        pad[plane, ROWS + tile_rows : ROWS + tile_rows + 1, :] = row_next[plane]
    tables = knot_tables(knot_ref, colour_ref, total_planes)
    sublane = lax.broadcasted_iota(jnp.int32, (ROWS, LANES), 0)
    lane = lax.broadcasted_iota(jnp.int32, (ROWS, LANES), 1)
    zero = jnp.zeros((ROWS, LANES), jnp.float32)
    cols = [slice(p * LANES, (p + 1) * LANES) for p in range(pieces)]
    toward = [jnp.broadcast_to(side_ref[:, c], (ROWS, LANES)) == 1 for c in cols]
    fetch(0).wait()

    def row_block(block, carry):
        @pl.when(block < blocks - 1)
        def _():
            fetch(block + 1).wait()

        own = pl.ds(pl.multiple_of(block * ROWS, ROWS), ROWS)
        mid = pl.ds(pl.multiple_of(block * ROWS + ROWS, ROWS), ROWS)
        up = pl.ds(pl.multiple_of(block * ROWS, ROWS), ROWS)
        down = pl.ds(pl.multiple_of(block * ROWS + 2 * ROWS, ROWS), ROWS)
        colour = [[zero] * pieces for _ in range(3)]
        passing = [zero + 1.0] * pieces
        for plane in range(planes):
            here = [pad[plane, mid, c] for c in cols]
            to_left = [pltpu.roll(v, LANES - 1, 1) for v in here] + [zero]
            to_right = [zero] + [pltpu.roll(v, 1, 1) for v in here]
            for p, c in enumerate(cols):
                x = here[p]
                before = above[0, own, c] if plane == 0 else pad[plane - 1, mid, c]
                after = below[0, own, c] if plane == planes - 1 else pad[plane + 1, mid, c]
                depth = after - before
                row_up = pltpu.roll(jnp.where(sublane == ROWS - 1, pad[plane, up, c], x), 1, 0)
                row_down = pltpu.roll(jnp.where(sublane == 0, pad[plane, down, c], x), ROWS - 1, 0)
                rows = row_down - row_up
                col_up = jnp.where(lane == 0, to_right[p], to_right[p + 1])
                col_down = jnp.where(lane == LANES - 1, to_left[p + 1], to_left[p])
                across = col_down - col_up
                facing = jnp.abs(0.448 * depth + 0.42 * rows + 0.336 * across)
                square = depth * depth + rows * rows + (across * across + 4.0)
                shading = 0.3 + facing * lax.rsqrt(square)
                red, green, blue, exponent = look_up(jnp.minimum(jnp.maximum(x, -3.0), 3.0), tables)
                passed = jnp.exp2(exponent)
                fade = jnp.where(toward[p], 1.0, passed)
                weight = jnp.where(toward[p], passing[p], 1.0) * ((1.0 - passed) * shading)
                for channel, value in enumerate((red, green, blue)):
                    colour[channel][p] = colour[channel][p] * fade + weight * value
                passing[p] = passing[p] * passed
        for channel, parts in enumerate(colour + [passing]):
            for p in range(pieces):
                first = block * (ROWS * 4 * pieces) + channel * pieces + p
                stage[pl.ds(first, ROWS, stride=4 * pieces), :] = parts[p]
        return carry

    lax.fori_loop(0, blocks, row_block, 0)
    core = core_ref[0]
    unit = 4 * pieces
    for pair in range(tile_rows // 2):
        kept = pl.multiple_of((pair * 2 + core) * unit, unit)
        sent = pl.multiple_of((pair * 2 + 1 - core) * unit, unit)
        keep_ref[pair] = stage[pl.ds(kept, unit), :]
        send_ref[pair] = stage[pl.ds(sent, unit), :]


def pair_kernel(core_ref, mine, other, side_ref, out):
    count, unit, lanes = mine.shape
    quarter = unit // 4
    front = jnp.concatenate([side_ref[...]] * 4, axis=0) + core_ref[0] == 1
    for k in range(count):
        a, b = mine[k], other[k]
        first, second = jnp.where(front, a, b), jnp.where(front, b, a)
        passing = first[3 * quarter :]
        lead = jnp.concatenate([passing] * 4, axis=0)
        base = jnp.concatenate([first[: 3 * quarter], jnp.zeros_like(passing)], axis=0)
        out[k] = base + lead * second


def final_kernel(parts, side_ref, out):
    count, unit, lanes = parts.shape
    quarter = unit // 4
    toward = side_ref[...] == 1
    colour = jnp.zeros((3 * quarter, lanes), jnp.float32)
    passing = jnp.ones((quarter, lanes), jnp.float32)
    for k in range(count):
        value = parts[k]
        passed = value[3 * quarter :]
        fade = jnp.where(toward, 1.0, passed)
        weight = jnp.where(toward, passing, 1.0)
        colour = colour * jnp.concatenate([fade] * 3, 0) + value[: 3 * quarter] * jnp.concatenate([weight] * 3, 0)
        passing = passing * passed
    out[...] = jnp.concatenate([colour, 1.0 - passing], axis=0)


def per_device(volume, knot_bins, colour_table, view_side):
    planes, tile_rows, columns = volume.shape
    slabs, tiles = lax.axis_size("slab"), lax.axis_size("tile")
    core = (lax.axis_index("slab") & 1).astype(jnp.int32).reshape(1)
    pieces = columns // LANES
    unit = 4 * pieces
    half = tile_rows // 2

    def shift(block, axis, size, step):
        route = [(i, i + step) for i in range(size) if 0 <= i + step < size]
        return lax.ppermute(block, axis, route)

    row_prev = shift(volume[:, tile_rows - 1 :, :], "tile", tiles, 1)
    row_next = shift(volume[:, :1, :], "tile", tiles, -1)
    above = shift(volume[planes - 1 :], "slab", slabs, 1)
    below = shift(volume[:1], "slab", slabs, -1)

    vmem = pl.BlockSpec(memory_space=pltpu.VMEM)
    smem = pl.BlockSpec(memory_space=pltpu.SMEM)
    hbm = pl.BlockSpec(memory_space=pltpu.HBM)
    side_lanes = view_side.reshape(pieces, LANES)
    part = jax.ShapeDtypeStruct((half, unit, LANES), jnp.float32)

    def march(*refs):
        march_kernel(planes * slabs, *refs)

    send, keep = pl.pallas_call(
        march,
        out_shape=[part, part],
        in_specs=[smem, smem, smem, hbm, vmem, vmem, vmem, vmem, vmem],
        out_specs=[vmem, vmem],
        scratch_shapes=[
            pltpu.VMEM((planes, tile_rows + 2 * ROWS, columns), jnp.float32),
            pltpu.VMEM((tile_rows * unit, LANES), jnp.float32),
            pltpu.SemaphoreType.DMA((tile_rows // ROWS,)),
        ],
        compiler_params=pltpu.CompilerParams(vmem_limit_bytes=24 << 20),
        name="march",
    )(core, knot_bins, colour_table, volume, above, below, row_prev, row_next, view_side.reshape(1, columns))
    got = lax.ppermute(send, "slab", [(i, i ^ 1) for i in range(slabs)])
    merged = pl.pallas_call(
        pair_kernel,
        out_shape=part,
        in_specs=[smem, vmem, vmem, vmem],
        out_specs=vmem,
        name="pair",
    )(core, keep, got, side_lanes)
    groups = [[2 * q + c for q in range(slabs // 2)] for c in range(2)]
    parts = lax.all_to_all(merged, "slab", 0, 0, axis_index_groups=groups, tiled=True)
    image = pl.pallas_call(
        final_kernel,
        out_shape=jax.ShapeDtypeStruct((unit, LANES), jnp.float32),
        in_specs=[vmem, vmem],
        out_specs=vmem,
        name="final",
    )(parts, side_lanes)
    return image.reshape(4, 1, 1, columns)


def solution(mesh):
    return jax.shard_map(
        per_device,
        mesh=mesh,
        in_specs=(P("slab", "tile", None), P(), P(), P()),
        out_specs=P(None, "slab", "tile", None),
        check_vma=False,
    )
```

time: 183 us -> 57.8 us (0.32)
  other arithmetic: 68 us -> 0 us
  between operations: 44.6 us -> 0.08 us
  blocking collectives: 0 us -> 24.4 us
  starting transfers between devices: 32.8 us -> 10.3 us
  local copies, waits for them, and re-layouts: 23.3 us -> 7.07 us
  Pallas kernels: 0 us -> 9.78 us
  waiting for transfers between devices: 12.7 us -> 5.4 us
    another operation x6 -> x0, other arithmetic: 62.3 us -> none  [the longest x3 55 us: sample_terms(): jnp.stack([(1.0 - passed) * totals[channel] * shading for channel in rang...]
    all_to_all x0 -> x1, blocking collectives: none -> 24.4 us  [per_device(): lax.all_to_all(merged, 'slab', 0, 0, axis_index_groups=groups, tiled=True)]
    ppermute x10 -> x5, starting transfers between devices: 32.8 us -> 10.3 us  [the longest x4 10.3 us: shift(): return lax.ppermute(block, axis, route)]
    slice x12 -> x2, local copies, waits for them, and re-layouts: 16.1 us -> 2.07 us  [the longest x1 1.08 us: per_device(): row_next = shift(volume[:, :1, :], 'tile', tiles, -1)]
    pallas_call x0 -> x3, Pallas kernels: none -> 9.78 us  [the longest x1 6.38 us: per_device(): pl.pallas_call(march, out_shape=[part, part], in_specs=[smem, smem, smem,...]
    ppermute x10 -> x5, waiting for transfers between devices: 12.7 us -> 5.4 us  [the longest x4 3.87 us: shift(): return lax.ppermute(block, axis, route)]
    rev x1 -> x0, local copies, waits for them, and re-layouts: 3.21 us -> none  [per_device(): backward_prod = jnp.flip(jnp.cumprod(jnp.flip(passed, 0), axis=0), 0)]
    select_n x13 -> x0, other arithmetic: 3.21 us -> none  [the longest x1 2.75 us: per_device(): weight = jnp.where(toward, ahead, behind)]
  transfers between devices with their start and end apart: 10 -> 5, of which waited for: 6 -> 2; matrix products, arithmetic and copies ran while one was open for 4% -> 2% of each run, Pallas kernels for 0% -> 0%
where the time goes in v1:
time: 57.8 us; the launch traced here: 57 us
  blocking collectives  24.4 us (42%)
  starting transfers between devices  10.3 us (18%)
  Pallas kernels  9.78 us (17%)
  local copies, waits for them, and re-layouts  7.07 us (12%)
  waiting for transfers between devices  5.4 us (9%)
    all_to_all x1, blocking collectives, per_device(): lax.all_to_all(merged, 'slab', 0, 0, axis_index_groups=groups, tiled=True)  24.4 us
    ppermute x4, starting transfers between devices, shift(): return lax.ppermute(block, axis, route)  10.3 us
    pallas_call x1, Pallas kernels, per_device(): pl.pallas_call(march, out_shape=[part, part], in_specs=[smem, smem, smem,...  6.38 us
    unnamed x12, local copies, waits for them, and re-layouts  5 us
    ppermute x4, waiting for transfers between devices, shift(): return lax.ppermute(block, axis, route)  3.87 us
    pallas_call x1, Pallas kernels, per_device(): pl.pallas_call(pair_kernel, out_shape=part, in_specs=[smem, vmem, vmem, v...  1.78 us
    pallas_call x1, Pallas kernels, per_device(): pl.pallas_call(final_kernel, out_shape=jax.ShapeDtypeStruct((unit, LANES)...  1.62 us
    ppermute x1, waiting for transfers between devices, per_device(): got = lax.ppermute(send, 'slab', [(i, i ^ 1) for i in range(slabs)])  1.53 us
  transfers between devices with their start and end apart: 5, of which 2 were waited for; matrix products, arithmetic and copies ran while one was open for 2% of the time, Pallas kernels for 0%

profile of v1, /device:TPU:8, one launch (start us, length us, event | category | flops | bytes accessed | tf_op | source)
XLA Modules:
  0.0 57.0 jit_solution(10246820433060800277)
XLA Ops:
  0.0 1.0 %fusion.1 = (f32[1,64,512]{2,1,0:T(8,128)S(1)}, f32[1,64,512]{2,1,0:T(8,128)S(1)}) fusion(f32[16,64,512]{2,1,0:T(8,128)} %refs_3_.1), kind=kLoop, calls=%fused_computation.1 | loop fusion | bytes 524288 | tf_op jit(solution)/shard_map/slice | solution.py:178
  1.0 1.3 %collective-permute-start.1 = (f32[1,64,512]{2,1,0:T(8,128)S(1)}, f32[1,64,512]{2,1,0:T(8,128)S(1)}, u32[]{:S(2)}, u32[]{:S(2)}) collective-permute-start(f32[1,64,512]{2,1,0:T(8,128)S(1)} %get-tuple-element.11), channel_id=1, source_target_pairs={{4,0},{8,4},{12,8},{16,12},{20,16},{24,20},{28,24},{32,28},{36,32}... | collective-permute-start | bytes 393224 | tf_op jit(solution)/shard_map/ppermute | solution.py:173
  2.3 3.0 %collective-permute-start = (f32[1,64,512]{2,1,0:T(8,128)S(1)}, f32[1,64,512]{2,1,0:T(8,128)S(1)}, u32[]{:S(2)}, u32[]{:S(2)}) collective-permute-start(f32[1,64,512]{2,1,0:T(8,128)S(1)} %get-tuple-element.12), channel_id=1, source_target_pairs={{0,4},{4,8},{8,12},{12,16},{16,20},{20,24},{24,28},{28,32},{32,36}... | collective-permute-start | bytes 393224 | tf_op jit(solution)/shard_map/ppermute | solution.py:173
  5.3 1.1 %fusion = (f32[16,1,512]{2,1,0:T(1,128)S(1)}, f32[16,1,512]{2,1,0:T(1,128)S(1)}) fusion(f32[16,64,512]{2,1,0:T(8,128)} %refs_3_.1), kind=kLoop, calls=%fused_computation | loop fusion | bytes 131072 | tf_op jit(solution)/shard_map/slice | solution.py:176
  6.4 4.1 %collective-permute-start.3 = (f32[16,1,512]{2,1,0:T(1,128)S(1)}, f32[16,1,512]{2,1,0:T(1,128)S(1)}, u32[]{:S(2)}, u32[]{:S(2)}) collective-permute-start(f32[16,1,512]{2,1,0:T(1,128)S(1)} %get-tuple-element.9), channel_id=1, source_target_pairs={{1,0},{2,1},{3,2},{5,4},{6,5},{7,6},{9,8},{10,9},{11,10},{13,12},{... | collective-permute-start | bytes 98312 | tf_op jit(solution)/shard_map/ppermute | solution.py:173
  10.5 1.9 %collective-permute-start.2 = (f32[16,1,512]{2,1,0:T(1,128)S(1)}, f32[16,1,512]{2,1,0:T(1,128)S(1)}, u32[]{:S(2)}, u32[]{:S(2)}) collective-permute-start(f32[16,1,512]{2,1,0:T(1,128)S(1)} %get-tuple-element.10), channel_id=1, source_target_pairs={{0,1},{1,2},{2,3},{4,5},{5,6},{6,7},{8,9},{9,10},{10,11},{12,13},{... | collective-permute-start | bytes 98312 | tf_op jit(solution)/shard_map/ppermute | solution.py:173
  12.5 0.0 collective-permute-done.3.refs_7_
  12.5 3.9 %collective-permute-done.2.refs_6_ = f32[16,1,512]{2,1,0:T(1,128)S(1)} collective-permute-done((f32[16,1,512]{2,1,0:T(1,128)S(1)}, f32[16,1,512]{2,1,0:T(1,128)S(1)}, u32[]{:S(2)}, u32[]{:S(2)}) %collective-permute-start.2) | collective-permute-done | bytes 32800 | tf_op jit(solution)/shard_map/ppermute | solution.py:173
  16.3 0.0 collective-permute-done.1.refs_5_
  16.3 0.0 collective-permute-done.refs_4_
  16.3 0.0 copy-start
  16.3 1.6 %copy-done = f32[16,64,512]{2,1,0:T(8,128)S(1)} copy-done((f32[16,64,512]{2,1,0:T(8,128)S(1)}, f32[16,64,512]{2,1,0:T(8,128)}, u32[]{:S(2)}) %copy-start) | copy-done | bytes 2097176
  17.9 0.0 copy-start.2
  17.9 0.7 %copy-done.2 = s32[512]{0:T(512)S(1)} copy-done((s32[512]{0:T(512)S(1)}, s32[512]{0:T(512)}, u32[]{:S(2)}) %copy-start.2) | copy-done | bytes 2072
  18.6 0.0 copy-start.3
  18.6 0.7 %copy-done.3 = f32[4,8]{1,0:T(4,128)S(1)} copy-done((f32[4,8]{1,0:T(4,128)S(1)}, f32[4,8]{1,0:T(4,128)}, u32[]{:S(2)}) %copy-start.3) | copy-done | bytes 152
  19.3 0.0 copy-start.4
  19.3 0.7 %copy-done.4 = s32[8]{0:T(128)S(1)} copy-done((s32[8]{0:T(128)S(1)}, s32[8]{0:T(128)}, u32[]{:S(2)}) %copy-start.4) | copy-done | bytes 56
  20.0 6.4 %march.1 = (f32[32,16,128]{2,1,0:T(8,128)S(1)}, f32[32,16,128]{2,1,0:T(8,128)S(1)}) custom-call(s32[1]{0:T(128)} %bitcast.refs_0_.core_ref, s32[8]{0:T(128)S(1)} %copy-done.4, f32[4,8]{1,0:T(4,128)S(1)} %copy-done.3, f32[16,64,512]{2,1,0:T(8,128)S(1)} %copy-done, f32[1,64,512]{2,1,0:T(8,128)S(1)} %collective-permute-done.refs_4_, ...), custom_call_target="tpu_custom_call" | custom-call | tf_op jit(solution)/shard_map/march/pallas_call | solution.py:189
  26.3 0.0 copy-start.1
  26.4 0.7 %copy-done.1 = f32[32,16,128]{2,1,0:T(8,128)} copy-done((f32[32,16,128]{2,1,0:T(8,128)}, f32[32,16,128]{2,1,0:T(8,128)S(1)}, u32[]{:S(2)}) %copy-start.1) | copy-done | bytes 262168
  27.0 0.0 collective-permute-start.4
  27.0 1.5 %collective-permute-done.4.other = f32[32,16,128]{2,1,0:T(8,128)S(1)} collective-permute-done((f32[32,16,128]{2,1,0:T(8,128)S(1)}, f32[32,16,128]{2,1,0:T(8,128)S(1)}, u32[]{:S(2)}, u32[]{:S(2)}) %collective-permute-start.4) | collective-permute-done | bytes 262176 | tf_op jit(solution)/shard_map/ppermute | solution.py:202
  28.6 0.0 copy-start.5
  28.6 0.7 %copy-done.5 = f32[32,16,128]{2,1,0:T(8,128)} copy-done((f32[32,16,128]{2,1,0:T(8,128)}, f32[32,16,128]{2,1,0:T(8,128)S(1)}, u32[]{:S(2)}) %copy-start.5) | copy-done | bytes 262168
  29.3 1.8 %pair.1 = f32[32,16,128]{2,1,0:T(8,128)} custom-call(s32[1]{0:T(128)} %bitcast.refs_0_.core_ref, f32[32,16,128]{2,1,0:T(8,128)} %copy-done.1, f32[32,16,128]{2,1,0:T(8,128)} %copy-done.5, s32[4,128]{1,0:T(4,128)} %bitcast.4), custom_call_target="tpu_custom_call" | custom-call | tf_op jit(solution)/shard_map/pair/pallas_call | solution.py:203
  31.1 24.4 %all_to_all.5.parts = f32[32,16,128]{2,1,0:T(8,128)} all-to-all(f32[32,16,128]{2,1,0:T(8,128)} %pair.1), channel_id=1, replica_groups={{0,8,16,24,32,40,48,56,64,72,80,88,96,104,112,120,128,136,144,152,160,1..., dimensions={0} | all-to-all | bytes 524288 | tf_op jit(solution)/shard_map/all_to_all | solution.py:211
  55.4 1.6 %final.1 = f32[16,128]{1,0:T(8,128)} custom-call(f32[32,16,128]{2,1,0:T(8,128)} %all_to_all.5.parts, s32[4,128]{1,0:T(4,128)} %bitcast.5), custom_call_target="tpu_custom_call" | custom-call | tf_op jit(solution)/shard_map/final/pallas_call | solution.py:212
Async XLA Ops:
  1.0 15.3 %collective-permute-start.1 = (f32[1,64,512]{2,1,0:T(8,128)S(1)}, f32[1,64,512]{2,1,0:T(8,128)S(1)}, u32[]{:S(2)}, u32[]{:S(2)}) collective-permute-start(f32[1,64,512]{2,1,0:T(8,128)S(1)} %get-tuple-element.11), channel_id=1, source_target_pairs={{4,0},{8,4},{12,8},{16,12},{20,16},{24,20},{28,24},{32,28},{36,32}... | collective-permute-start | bytes 393224 | tf_op jit(solution)/shard_map/ppermute | solution.py:173
  2.3 14.0 %collective-permute-start = (f32[1,64,512]{2,1,0:T(8,128)S(1)}, f32[1,64,512]{2,1,0:T(8,128)S(1)}, u32[]{:S(2)}, u32[]{:S(2)}) collective-permute-start(f32[1,64,512]{2,1,0:T(8,128)S(1)} %get-tuple-element.12), channel_id=1, source_target_pairs={{0,4},{4,8},{8,12},{12,16},{16,20},{20,24},{24,28},{28,32},{32,36}... | collective-permute-start | bytes 393224 | tf_op jit(solution)/shard_map/ppermute | solution.py:173
  6.4 6.0 %collective-permute-start.3 = (f32[16,1,512]{2,1,0:T(1,128)S(1)}, f32[16,1,512]{2,1,0:T(1,128)S(1)}, u32[]{:S(2)}, u32[]{:S(2)}) collective-permute-start(f32[16,1,512]{2,1,0:T(1,128)S(1)} %get-tuple-element.9), channel_id=1, source_target_pairs={{1,0},{2,1},{3,2},{5,4},{6,5},{7,6},{9,8},{10,9},{11,10},{13,12},{... | collective-permute-start | bytes 98312 | tf_op jit(solution)/shard_map/ppermute | solution.py:173
  10.5 5.8 %collective-permute-start.2 = (f32[16,1,512]{2,1,0:T(1,128)S(1)}, f32[16,1,512]{2,1,0:T(1,128)S(1)}, u32[]{:S(2)}, u32[]{:S(2)}) collective-permute-start(f32[16,1,512]{2,1,0:T(1,128)S(1)} %get-tuple-element.10), channel_id=1, source_target_pairs={{0,1},{1,2},{2,3},{4,5},{5,6},{6,7},{8,9},{9,10},{10,11},{12,13},{... | collective-permute-start | bytes 98312 | tf_op jit(solution)/shard_map/ppermute | solution.py:173
  16.3 1.6 %copy-start = (f32[16,64,512]{2,1,0:T(8,128)S(1)}, f32[16,64,512]{2,1,0:T(8,128)}, u32[]{:S(2)}) copy-start(f32[16,64,512]{2,1,0:T(8,128)} %refs_3_.1) | copy-start | bytes 6291460
  17.9 0.7 %copy-start.2 = (s32[512]{0:T(512)S(1)}, s32[512]{0:T(512)}, u32[]{:S(2)}) copy-start(s32[512]{0:T(512)} %param.7) | copy-start | bytes 6148
  18.6 0.7 %copy-start.3 = (f32[4,8]{1,0:T(4,128)S(1)}, f32[4,8]{1,0:T(4,128)}, u32[]{:S(2)}) copy-start(f32[4,8]{1,0:T(4,128)} %refs_2_.1) | copy-start | bytes 388
  19.3 0.7 %copy-start.4 = (s32[8]{0:T(128)S(1)}, s32[8]{0:T(128)}, u32[]{:S(2)}) copy-start(s32[8]{0:T(128)} %refs_1_.1) | copy-start | bytes 100
  26.3 0.7 %copy-start.1 = (f32[32,16,128]{2,1,0:T(8,128)}, f32[32,16,128]{2,1,0:T(8,128)S(1)}, u32[]{:S(2)}) copy-start(f32[32,16,128]{2,1,0:T(8,128)S(1)} %get-tuple-element.7.mine) | copy-start | bytes 786436
  27.0 1.5 %collective-permute-start.4 = (f32[32,16,128]{2,1,0:T(8,128)S(1)}, f32[32,16,128]{2,1,0:T(8,128)S(1)}, u32[]{:S(2)}, u32[]{:S(2)}) collective-permute-start(f32[32,16,128]{2,1,0:T(8,128)S(1)} %get-tuple-element.8), channel_id=1, source_target_pairs={{0,4},{4,0},{8,12},{12,8},{16,20},{20,16},{24,28},{28,24},{32,36},... | collective-permute-start | bytes 786440 | tf_op jit(solution)/shard_map/ppermute | solution.py:202
  28.6 0.7 %copy-start.5 = (f32[32,16,128]{2,1,0:T(8,128)}, f32[32,16,128]{2,1,0:T(8,128)S(1)}, u32[]{:S(2)}) copy-start(f32[32,16,128]{2,1,0:T(8,128)S(1)} %collective-permute-done.4.other) | copy-start | bytes 786436

commit v2 on v1

v2 whole, which is shorter than its diff:
```python
import jax
import jax.numpy as jnp
from jax import lax
from jax.experimental import pallas as pl
from jax.experimental.pallas import tpu as pltpu
from jax.sharding import PartitionSpec as P

BINS = 256
KNOTS = 8
LOG2_E = 1.4426950408889634
LANES = 128
ROWS = 8
SMALL_VMEM = 4 << 20


def knot_tables(knot_bins, colour_table, total_planes):
    sublane = lax.broadcasted_iota(jnp.int32, (ROWS, LANES), 0)

    def spread(read):
        table = jnp.full((ROWS, LANES), read(0), jnp.float32)
        for knot in range(1, KNOTS):
            table = jnp.where(sublane == knot, read(knot), table)
        return table

    scale = 6.0 / (BINS - 1)
    knot_at = spread(lambda knot: knot_bins[knot].astype(jnp.float32)) * scale - 3.0
    knot_at = jnp.where(sublane == KNOTS - 1, 3.0, knot_at)
    width = pltpu.roll(knot_at, KNOTS - 1, 0) - knot_at
    starts, slopes = [], []
    for channel in range(4):
        start = spread(lambda knot: colour_table[channel, knot])
        rise = (pltpu.roll(start, KNOTS - 1, 0) - start) / width
        slope = jnp.where(sublane == KNOTS - 1, 0.0, rise)
        factor = -400.0 / total_planes * LOG2_E if channel == 3 else 1.0
        starts.append(start * factor)
        slopes.append(slope * factor)
    return [knot_at] + starts + slopes


def look_up(value, tables, edges):
    index = jnp.zeros(value.shape, jnp.int32)
    for knot in range(1, KNOTS):
        index = jnp.where(value >= edges[knot], knot, index)

    def pick(table):
        return jnp.take_along_axis(table, index, axis=0, mode="promise_in_bounds")

    offset = value - pick(tables[0])
    return [pick(tables[1 + c]) + offset * pick(tables[5 + c]) for c in range(4)]


def low_bits(axis, *bits):
    index = lax.axis_index(axis)
    return [(index >> bit) & 1 for bit in bits]


def load_kernel(
    total_planes, volume, knots_hbm, colours_hbm, side_hbm,
    pad, plane_near, plane_far, row_near, row_far, tables_ref, side_ref, knot_ref, colour_ref, sems, small_sems,
):
    planes, tile_rows, columns = volume.shape
    pieces = columns // LANES
    (core,), (tile,) = low_bits("slab", 0), low_bits("tile", 0)
    small = [
        pltpu.make_async_copy(knots_hbm, knot_ref, small_sems.at[0]),
        pltpu.make_async_copy(colours_hbm, colour_ref, small_sems.at[1]),
        pltpu.make_async_copy(side_hbm, side_ref, small_sems.at[2]),
    ]
    for copy in small:
        copy.start()
    fetches = []
    for plane in range(planes):
        for p in range(pieces):
            first = pad_row(pieces, tile_rows, plane + 1, p, 0)
            source = volume.at[plane, :, pl.ds(p * LANES, LANES)]
            sem = sems.at[plane * pieces + p]
            fetches.append(pltpu.make_async_copy(source, pad.at[pl.ds(first, tile_rows)], sem))
    for fetch in fetches:
        fetch.start()
    for copy in small:
        copy.wait()
    for k, table in enumerate(knot_tables(knot_ref, colour_ref, total_planes)):
        tables_ref[k] = table
    for fetch in fetches:
        fetch.wait()
    for k in range(planes * pieces // ROWS):
        first = pad_row(pieces, tile_rows, 1, k * ROWS, 0)
        stride = tile_rows + 2 * ROWS
        row_near[k] = pad[pl.ds(first + (tile_rows - 1) * (1 - tile), ROWS, stride=stride), :]
        row_far[k] = pad[pl.ds(first + (tile_rows - 1) * tile, ROWS, stride=stride), :]
    for p in range(pieces):
        near = pad_row(pieces, tile_rows, 1 + (planes - 1) * (1 - core), p, 0)
        far = pad_row(pieces, tile_rows, 1 + (planes - 1) * core, p, 0)
        plane_near[p] = pad[pl.ds(pl.multiple_of(near, ROWS), tile_rows), :]
        plane_far[p] = pad[pl.ds(pl.multiple_of(far, ROWS), tile_rows), :]


def pad_row(pieces, tile_rows, plane, piece, row):
    return (plane * pieces + piece) * (tile_rows + 2 * ROWS) + ROWS + row


def add_halo(pad, plane_near, plane_far, row_near, row_far):
    pieces, tile_rows, _ = plane_near.shape
    planes = row_near.shape[0] * ROWS // pieces
    (core,), (tile,) = low_bits("slab", 0), low_bits("tile", 0)
    for p in range(pieces):
        near = pad_row(pieces, tile_rows, (planes + 1) * (1 - core), p, 0)
        far = pad_row(pieces, tile_rows, (planes + 1) * core, p, 0)
        pad[pl.ds(pl.multiple_of(near, ROWS), tile_rows), :] = plane_near[p]
        pad[pl.ds(pl.multiple_of(far, ROWS), tile_rows), :] = plane_far[p]
    for k in range(row_near.shape[0]):
        first = pad_row(pieces, tile_rows, 1, k * ROWS, -1)
        stride = tile_rows + 2 * ROWS
        pad[pl.ds(first + (tile_rows + 1) * (1 - tile), ROWS, stride=stride), :] = row_near[k]
        pad[pl.ds(first + (tile_rows + 1) * tile, ROWS, stride=stride), :] = row_far[k]


def march(pad, tables_ref, side_ref, out, first_row, step, count):
    pieces = side_ref.shape[1] // LANES
    tile_rows = ROWS * ROWS
    planes = pad.shape[0] // (tile_rows + 2 * ROWS) // pieces - 2
    tables = [tables_ref[k] for k in range(tables_ref.shape[0])]
    edges = [jnp.broadcast_to(tables[0][k : k + 1], (ROWS, LANES)) for k in range(KNOTS)]
    lane = lax.broadcasted_iota(jnp.int32, (ROWS, LANES), 1)
    zero = jnp.zeros((ROWS, LANES), jnp.float32)
    cols = [slice(p * LANES, (p + 1) * LANES) for p in range(pieces)]
    toward = [jnp.broadcast_to(side_ref[:, c], (ROWS, LANES)) == 1 for c in cols]

    def group(j, carry):
        def read(plane, piece, shift=0):
            row = pad_row(pieces, tile_rows, plane, piece, first_row + step * j + shift)
            return pad[pl.ds(row, ROWS, stride=ROWS), :]

        colour = [[zero] * pieces for _ in range(3)]
        passing = [zero + 1.0] * pieces
        for plane in range(1, planes + 1):
            here = [read(plane, p) for p in range(pieces)]
            to_left = [pltpu.roll(v, LANES - 1, 1) for v in here] + [zero]
            to_right = [zero] + [pltpu.roll(v, 1, 1) for v in here]
            for p in range(pieces):
                x = here[p]
                depth = read(plane + 1, p) - read(plane - 1, p)
                rows = read(plane, p, 1) - read(plane, p, -1)
                col_up = jnp.where(lane == 0, to_right[p], to_right[p + 1])
                col_down = jnp.where(lane == LANES - 1, to_left[p + 1], to_left[p])
                across = col_down - col_up
                facing = jnp.abs(0.448 * depth + 0.42 * rows + 0.336 * across)
                square = depth * depth + rows * rows + (across * across + 4.0)
                shading = 0.3 + facing * lax.rsqrt(square)
                clipped = jnp.minimum(jnp.maximum(x, -3.0), 3.0)
                red, green, blue, exponent = look_up(clipped, tables, edges)
                passed = jnp.exp2(exponent)
                fade = jnp.where(toward[p], 1.0, passed)
                weight = jnp.where(toward[p], passing[p], 1.0) * ((1.0 - passed) * shading)
                for channel, value in enumerate((red, green, blue)):
                    colour[channel][p] = colour[channel][p] * fade + weight * value
                passing[p] = passing[p] * passed
        for channel, parts in enumerate(colour + [passing]):
            for p, c in enumerate(cols):
                out[j, channel, :, c] = parts[p]
        return carry

    lax.fori_loop(0, count, group, 0)


def merge(first_is_front, mine, other):
    lead = jnp.where(first_is_front, mine[3], other[3])
    merged = [
        jnp.where(first_is_front, mine[c], other[c]) + lead * jnp.where(first_is_front, other[c], mine[c])
        for c in range(3)
    ]
    return merged + [mine[3] * other[3]]


def both_halves(value):
    sublane = lax.broadcasted_iota(jnp.int32, value.shape, 0)
    return jnp.where(sublane < 4, pltpu.roll(value, 4, 0), value)


def final_kernel(parts, side_ref, out):
    toward = jnp.concatenate([side_ref[...]] * 2, axis=0) == 1
    lower = lax.broadcasted_iota(jnp.int32, (ROWS, LANES), 0) < 4
    top = bottom = jnp.zeros((ROWS, LANES), jnp.float32)
    passing = jnp.ones((ROWS, LANES), jnp.float32)
    for k in range(parts.shape[0]):
        passed = both_halves(parts[k, ROWS:])
        fade = jnp.where(toward, 1.0, passed)
        weight = jnp.where(toward, passing, 1.0)
        top = top * fade + parts[k, :ROWS] * weight
        bottom = bottom * fade + parts[k, ROWS:] * weight
        passing = passing * passed
    out[:ROWS] = top
    out[ROWS:] = jnp.where(lower, bottom, 1.0 - passing)


def per_device(volume, knot_bins, colour_table, view_side):
    planes, tile_rows, columns = volume.shape
    slabs, tiles = lax.axis_size("slab"), lax.axis_size("tile")
    pieces = columns // LANES
    unit = 4 * pieces
    groups = ROWS // 2

    vmem = pl.BlockSpec(memory_space=pltpu.VMEM)
    hbm = pl.BlockSpec(memory_space=pltpu.HBM)
    small = pltpu.CompilerParams(vmem_limit_bytes=SMALL_VMEM)

    def array(*shape):
        return jax.ShapeDtypeStruct(shape, jnp.float32)

    inputs = (volume, knot_bins, colour_table, view_side.reshape(1, columns))
    pad, *edges, tables, side = pl.pallas_call(
        lambda *refs: load_kernel(planes * slabs, *refs),
        out_shape=[
            pltpu.VMEM(((planes + 2) * pieces * (tile_rows + 2 * ROWS), LANES), jnp.float32),
            *[pltpu.VMEM((pieces, tile_rows, LANES), jnp.float32)] * 2,
            *[pltpu.VMEM((planes * pieces // ROWS, ROWS, LANES), jnp.float32)] * 2,
            pltpu.VMEM((9, ROWS, LANES), jnp.float32),
            pltpu.VMEM((1, columns), jnp.int32),
        ],
        in_specs=[hbm] * 4,
        out_specs=[vmem] * 7,
        scratch_shapes=[
            pltpu.SMEM((KNOTS,), jnp.int32),
            pltpu.SMEM((4, KNOTS), jnp.float32),
            pltpu.SemaphoreType.DMA((planes * pieces,)),
            pltpu.SemaphoreType.DMA((3,)),
        ],
        compiler_params=pltpu.CompilerParams(vmem_limit_bytes=SMALL_VMEM),
        name="load",
    )(*[pltpu.with_memory_space_constraint(x, pltpu.HBM) for x in inputs])

    def swap(block, axis, size, low):
        route = [(i, i + 1) for i in range(low, size - 1, 2)]
        return lax.ppermute(block, axis, route + [(j, i) for i, j in route])

    halo = [
        swap(edges[0], "slab", slabs, 0),
        swap(edges[1], "slab", slabs, 1),
        swap(edges[2], "tile", tiles, 0),
        swap(edges[3], "tile", tiles, 1),
    ]

    def cost(share):
        count = planes * tile_rows * columns // share
        return pl.CostEstimate(flops=100 * count, bytes_accessed=16 * count, transcendentals=2 * count)

    def march_sent(pad_in, near, far, row_near, row_far, tables, side, pad, out):
        add_halo(pad, near, far, row_near, row_far)
        (core,) = low_bits("slab", 0)
        march(pad, tables, side, out, 1 - core, 2, groups)

    def march_kept(pad, tables, side, out):
        (core,) = low_bits("slab", 0)
        march(pad, tables, side, out, core, 2, groups)

    half = array(groups, 4, ROWS, columns)
    pad, sent = pl.pallas_call(
        march_sent,
        out_shape=[array(*pad.shape), half],
        in_specs=[vmem] * 7,
        out_specs=[vmem] * 2,
        input_output_aliases={0: 0},
        compiler_params=small,
        cost_estimate=cost(2),
        name="march_sent",
    )(pad, *halo, tables, side)
    got = lax.ppermute(sent, "slab", [(i, i ^ 1) for i in range(slabs)])
    kept = pl.pallas_call(
        march_kept,
        out_shape=half,
        in_specs=[vmem] * 3,
        out_specs=vmem,
        compiler_params=small,
        cost_estimate=cost(2),
        name="march_kept",
    )(pad, tables, side)

    def pair(mine, other, side_ref, out):
        (core,) = low_bits("slab", 0)
        for p in range(pieces):
            c = slice(p * LANES, (p + 1) * LANES)
            front = jnp.broadcast_to(side_ref[:, c], (ROWS, LANES)) + core == 1
            for x in range(groups):
                whole = merge(front, [mine[x, k, :, c] for k in range(4)], [other[x, k, :, c] for k in range(4)])
                for k, value in enumerate(whole):
                    out[pl.ds(x * unit + k * pieces + p, ROWS, stride=groups * unit), :] = value

    merged = pl.pallas_call(
        pair,
        out_shape=array(ROWS * groups * unit, LANES),
        in_specs=[vmem] * 3,
        out_specs=vmem,
        compiler_params=small,
        name="pair",
    )(kept, got, side)
    members = [[2 * q + c for q in range(slabs // 2)] for c in range(2)]
    parts = lax.all_to_all(
        merged.reshape(slabs // 2, unit, LANES), "slab", 0, 0, axis_index_groups=members, tiled=True
    )
    image = pl.pallas_call(
        final_kernel,
        out_shape=array(unit, LANES),
        in_specs=[vmem] * 2,
        out_specs=vmem,
        compiler_params=small,
        name="final",
    )(parts, side.reshape(pieces, LANES))
    return image.reshape(4, 1, 1, columns)


def solution(mesh):
    return jax.shard_map(
        per_device,
        mesh=mesh,
        in_specs=(P("slab", "tile", None), P(), P(), P()),
        out_specs=P(None, "slab", "tile", None),
        check_vma=False,
    )
```

time: 57.8 us -> 43.4 us (0.75)
  local copies, waits for them, and re-layouts: 7.07 us -> 0 us
  starting transfers between devices: 10.3 us -> 6.05 us
  waiting for transfers between devices: 5.4 us -> 3.22 us
  Pallas kernels: 9.78 us -> 8.34 us
  blocking collectives: 24.4 us -> 25.1 us
    unnamed x12 -> x0, local copies, waits for them, and re-layouts: 5 us -> none
    ppermute x5, starting transfers between devices: 10.3 us -> 6.05 us  [the longest x4 5.6 us: swap(): return lax.ppermute(block, axis, route + [(j, i) for i, j in route])]
    ppermute x5, waiting for transfers between devices: 5.4 us -> 3.22 us  [the longest x4 3.21 us: swap(): return lax.ppermute(block, axis, route + [(j, i) for i, j in route])]
    slice x2 -> x0, local copies, waits for them, and re-layouts: 2.07 us -> none  [the longest x1 1.08 us: per_device(): row_next = shift(volume[:, :1, :], 'tile', tiles, -1)]
    pallas_call x3 -> x5, Pallas kernels: 9.78 us -> 8.34 us  [the longest x1 2.69 us: per_device(): pl.pallas_call(march_sent, out_shape=[array(*pad.shape), half], in_specs=...]
    all_to_all x1, blocking collectives: 24.4 us -> 25.1 us  [per_device(): lax.all_to_all(merged.reshape(slabs // 2, unit, LANES), 'slab', 0, 0, axi...]
  transfers between devices with their start and end apart: 5 -> 5, of which waited for: 2 -> 1; matrix products, arithmetic and copies ran while one was open for 2% -> 0% of each run, Pallas kernels for 0% -> 6%
where the time goes in v2:
time: 43.4 us; the launch traced here: 42.7 us
  blocking collectives  25.1 us (58%)
  Pallas kernels  8.34 us (19%)
  starting transfers between devices  6.05 us (14%)
  waiting for transfers between devices  3.22 us (7%)
    all_to_all x1, blocking collectives, per_device(): lax.all_to_all(merged.reshape(slabs // 2, unit, LANES), 'slab', 0, 0, axi...  25.1 us
    ppermute x4, starting transfers between devices, swap(): return lax.ppermute(block, axis, route + [(j, i) for i, j in route])  5.6 us
    ppermute x4, waiting for transfers between devices, swap(): return lax.ppermute(block, axis, route + [(j, i) for i, j in route])  3.21 us
    pallas_call x1, Pallas kernels, per_device(): pl.pallas_call(march_sent, out_shape=[array(*pad.shape), half], in_specs=...  2.69 us
    pallas_call x1, Pallas kernels, per_device(): pl.pallas_call(march_kept, out_shape=half, in_specs=[vmem] * 3, out_specs...  2.64 us
    pallas_call x1, Pallas kernels, per_device(): pl.pallas_call(lambda *refs: load_kernel(planes * slabs, *refs), out_shap...  2.18 us
  transfers between devices with their start and end apart: 5, of which 1 were waited for; matrix products, arithmetic and copies ran while one was open for 0% of the time, Pallas kernels for 6%

profile of v2, /device:TPU:8, one launch (start us, length us, event | category | flops | bytes accessed | tf_op | source)
XLA Modules:
  0.0 42.7 jit_solution(1169413071237192340)
XLA Ops:
  0.0 2.2 %load.1 = (f32[5760,128]{1,0:T(8,128)S(1)}, f32[4,64,128]{2,1,0:T(8,128)S(1)}, f32[4,64,128]{2,1,0:T(8,128)S(1)}, f32[8,8,128]{2,1,0:T(8,128)S(1)}, f32[8,8,128]...) custom-call(f32[16,64,512]{2,1,0:T(8,128)} %refs_0_.1, s32[8]{0:T(128)} %refs_1_.1, f32[4,8]{1,0:T(4,128)} %refs_2_.1, ...), custom_call_target="tpu_custom_call" | custom-call | tf_op jit(solution)/shard_map/load/pallas_call | solution.py:211
  2.2 0.1 collective-permute-start
  2.3 0.7 %collective-permute-start.1 = (f32[4,64,128]{2,1,0:T(8,128)S(1)}, f32[4,64,128]{2,1,0:T(8,128)S(1)}, u32[]{:S(2)}, u32[]{:S(2)}) collective-permute-start(f32[4,64,128]{2,1,0:T(8,128)S(1)} %get-tuple-element.16), channel_id=1, source_target_pairs={{4,8},{12,16},{20,24},{28,32},{36,40},{44,48},{52,56},{60,64},{68,... | collective-permute-start | bytes 393224 | tf_op jit(solution)/shard_map/ppermute | solution.py:234
  3.0 2.3 %collective-permute-start.2 = (f32[8,8,128]{2,1,0:T(8,128)S(1)}, f32[8,8,128]{2,1,0:T(8,128)S(1)}, u32[]{:S(2)}, u32[]{:S(2)}) collective-permute-start(f32[8,8,128]{2,1,0:T(8,128)S(1)} %get-tuple-element.17), channel_id=1, source_target_pairs={{0,1},{2,3},{1,0},{3,2},{4,5},{6,7},{5,4},{7,6},{8,9},{10,11},{9,8... | collective-permute-start | bytes 98312 | tf_op jit(solution)/shard_map/ppermute | solution.py:234
  5.2 2.6 %collective-permute-start.3 = (f32[8,8,128]{2,1,0:T(8,128)S(1)}, f32[8,8,128]{2,1,0:T(8,128)S(1)}, u32[]{:S(2)}, u32[]{:S(2)}) collective-permute-start(f32[8,8,128]{2,1,0:T(8,128)S(1)} %get-tuple-element.18), channel_id=1, source_target_pairs={{1,2},{2,1},{5,6},{6,5},{9,10},{10,9},{13,14},{14,13},{17,18},{18,... | collective-permute-start | bytes 98312 | tf_op jit(solution)/shard_map/ppermute | solution.py:234
  7.8 0.0 collective-permute-done.2.row_near
  7.8 3.2 %collective-permute-done.3.row_far = f32[8,8,128]{2,1,0:T(8,128)S(1)} collective-permute-done((f32[8,8,128]{2,1,0:T(8,128)S(1)}, f32[8,8,128]{2,1,0:T(8,128)S(1)}, u32[]{:S(2)}, u32[]{:S(2)}) %collective-permute-start.3) | collective-permute-done | bytes 32800 | tf_op jit(solution)/shard_map/ppermute | solution.py:234
  11.0 0.0 collective-permute-done.near
  11.0 0.0 collective-permute-done.1.far
  11.0 2.7 %march_sent.1 = (f32[5760,128]{1,0:T(8,128)S(1)}, f32[4,4,8,512]{3,2,1,0:T(8,128)S(1)}) custom-call(f32[5760,128]{1,0:T(8,128)S(1)} %get-tuple-element.14.pad_in, f32[4,64,128]{2,1,0:T(8,128)S(1)} %collective-permute-done.near, f32[4,64,128]{2,1,0:T(8,128)S(1)} %collective-permute-done.1.far, ...), custom_call_target="tpu_custom_call", output_to_operand_aliasing={{0}: (0, {})} | custom-call | flops 26214400 | bytes 4194304 | tf_op jit(solution)/shard_map/march_sent/pallas_call | solution.py:257
  13.7 0.4 %collective-permute-start.4 = (f32[4,4,8,512]{3,2,1,0:T(8,128)S(1)}, f32[4,4,8,512]{3,2,1,0:T(8,128)S(1)}, u32[]{:S(2)}, u32[]{:S(2)}) collective-permute-start(f32[4,4,8,512]{3,2,1,0:T(8,128)S(1)} %get-tuple-element.22), channel_id=1, source_target_pairs={{0,4},{4,0},{8,12},{12,8},{16,20},{20,16},{24,28},{28,24},{32,36},... | collective-permute-start | bytes 786440 | tf_op jit(solution)/shard_map/ppermute | solution.py:267
  14.2 2.6 %march_kept.1.mine = f32[4,4,8,512]{3,2,1,0:T(8,128)S(1)} custom-call(f32[5760,128]{1,0:T(8,128)S(1)} %get-tuple-element.21.pad, f32[9,8,128]{2,1,0:T(8,128)S(1)} %get-tuple-element.19.tables, s32[1,512]{1,0:T(1,128)S(1)} %get-tuple-element.20.side.side_ref), custom_call_target="tpu_custom_call" | custom-call | flops 26214400 | bytes 4194304 | tf_op jit(solution)/shard_map/march_kept/pallas_call | solution.py:268
  16.8 0.0 collective-permute-done.4.other
  16.8 0.2 pair.1
  17.0 25.1 %all_to_all.5.parts = f32[32,16,128]{2,1,0:T(8,128)S(1)} all-to-all(f32[32,16,128]{2,1,0:T(8,128)S(1)} %bitcast.4), channel_id=1, replica_groups={{0,8,16,24,32,40,48,56,64,72,80,88,96,104,112,120,128,136,144,152,160,1..., dimensions={0} | all-to-all | bytes 524288 | tf_op jit(solution)/shard_map/all_to_all | solution.py:297
  42.1 0.7 %final.1 = f32[16,128]{1,0:T(8,128)} custom-call(f32[32,16,128]{2,1,0:T(8,128)S(1)} %all_to_all.5.parts, s32[4,128]{1,0:T(4,128)S(1)} %bitcast.5), custom_call_target="tpu_custom_call" | custom-call | tf_op jit(solution)/shard_map/final/pallas_call | solution.py:300
Async XLA Ops:
  2.2 8.8 %collective-permute-start = (f32[4,64,128]{2,1,0:T(8,128)S(1)}, f32[4,64,128]{2,1,0:T(8,128)S(1)}, u32[]{:S(2)}, u32[]{:S(2)}) collective-permute-start(f32[4,64,128]{2,1,0:T(8,128)S(1)} %get-tuple-element.15), channel_id=1, source_target_pairs={{0,4},{8,12},{16,20},{24,28},{32,36},{40,44},{48,52},{56,60},{64,6... | collective-permute-start | bytes 393224 | tf_op jit(solution)/shard_map/ppermute | solution.py:234
  2.3 8.8 %collective-permute-start.1 = (f32[4,64,128]{2,1,0:T(8,128)S(1)}, f32[4,64,128]{2,1,0:T(8,128)S(1)}, u32[]{:S(2)}, u32[]{:S(2)}) collective-permute-start(f32[4,64,128]{2,1,0:T(8,128)S(1)} %get-tuple-element.16), channel_id=1, source_target_pairs={{4,8},{12,16},{20,24},{28,32},{36,40},{44,48},{52,56},{60,64},{68,... | collective-permute-start | bytes 393224 | tf_op jit(solution)/shard_map/ppermute | solution.py:234
  3.0 4.9 %collective-permute-start.2 = (f32[8,8,128]{2,1,0:T(8,128)S(1)}, f32[8,8,128]{2,1,0:T(8,128)S(1)}, u32[]{:S(2)}, u32[]{:S(2)}) collective-permute-start(f32[8,8,128]{2,1,0:T(8,128)S(1)} %get-tuple-element.17), channel_id=1, source_target_pairs={{0,1},{2,3},{1,0},{3,2},{4,5},{6,7},{5,4},{7,6},{8,9},{10,11},{9,8... | collective-permute-start | bytes 98312 | tf_op jit(solution)/shard_map/ppermute | solution.py:234
  5.2 5.8 %collective-permute-start.3 = (f32[8,8,128]{2,1,0:T(8,128)S(1)}, f32[8,8,128]{2,1,0:T(8,128)S(1)}, u32[]{:S(2)}, u32[]{:S(2)}) collective-permute-start(f32[8,8,128]{2,1,0:T(8,128)S(1)} %get-tuple-element.18), channel_id=1, source_target_pairs={{1,2},{2,1},{5,6},{6,5},{9,10},{10,9},{13,14},{14,13},{17,18},{18,... | collective-permute-start | bytes 98312 | tf_op jit(solution)/shard_map/ppermute | solution.py:234
  13.7 3.1 %collective-permute-start.4 = (f32[4,4,8,512]{3,2,1,0:T(8,128)S(1)}, f32[4,4,8,512]{3,2,1,0:T(8,128)S(1)}, u32[]{:S(2)}, u32[]{:S(2)}) collective-permute-start(f32[4,4,8,512]{3,2,1,0:T(8,128)S(1)} %get-tuple-element.22), channel_id=1, source_target_pairs={{0,4},{4,0},{8,12},{12,8},{16,20},{20,16},{24,28},{28,24},{32,36},... | collective-permute-start | bytes 786440 | tf_op jit(solution)/shard_map/ppermute | solution.py:267

commit v3 on v2

v3 whole, which is shorter than its diff:
```python
import jax
import jax.numpy as jnp
from jax import lax
from jax.experimental import pallas as pl
from jax.experimental.pallas import tpu as pltpu
from jax.sharding import PartitionSpec as P

BINS = 256
KNOTS = 8
LOG2_E = 1.4426950408889634
LANES = 128
ROWS = 8
SMALL_VMEM = 4 << 20
LOAD_PARTS = 1
INNER_UNROLL = 2


def knot_tables(knot_bins, colour_table, total_planes):
    sublane = lax.broadcasted_iota(jnp.int32, (ROWS, LANES), 0)

    def spread(read):
        table = jnp.full((ROWS, LANES), read(0), jnp.float32)
        for knot in range(1, KNOTS):
            table = jnp.where(sublane == knot, read(knot), table)
        return table

    scale = 6.0 / (BINS - 1)
    knot_at = spread(lambda knot: knot_bins[knot].astype(jnp.float32)) * scale - 3.0
    knot_at = jnp.where(sublane == KNOTS - 1, 3.0, knot_at)
    width = pltpu.roll(knot_at, KNOTS - 1, 0) - knot_at
    starts, slopes = [], []
    for channel in range(4):
        start = spread(lambda knot: colour_table[channel, knot])
        rise = (pltpu.roll(start, KNOTS - 1, 0) - start) / width
        slope = jnp.where(sublane == KNOTS - 1, 0.0, rise)
        factor = -400.0 / total_planes * LOG2_E if channel == 3 else 1.0
        starts.append(start * factor)
        slopes.append(slope * factor)
    return [knot_at] + starts + slopes


def look_up(value, tables, edges):
    index = jnp.zeros(value.shape, jnp.int32)
    for knot in range(1, KNOTS - 1):
        index = jnp.where(value >= edges[knot], knot, index)

    def pick(table):
        return jnp.take_along_axis(table, index, axis=0, mode="promise_in_bounds")

    offset = value - pick(tables[0])
    return [pick(tables[1 + c]) + offset * pick(tables[5 + c]) for c in range(4)]


def low_bits(axis, *bits):
    index = lax.axis_index(axis)
    return [(index >> bit) & 1 for bit in bits]


def load_kernel(
    total_planes, volume, knots_hbm, colours_hbm, side_hbm,
    pad, plane_near, plane_far, row_near, row_far, tables_ref, side_ref, knot_ref, colour_ref, sems, small_sems,
):
    planes, tile_rows, columns = volume.shape
    pieces = columns // LANES
    (core,), (tile,) = low_bits("slab", 0), low_bits("tile", 0)
    small = [
        pltpu.make_async_copy(knots_hbm, knot_ref, small_sems.at[0]),
        pltpu.make_async_copy(colours_hbm, colour_ref, small_sems.at[1]),
        pltpu.make_async_copy(side_hbm, side_ref, small_sems.at[2]),
    ]
    fetches = []
    share = planes // LOAD_PARTS
    for k in range(LOAD_PARTS):
        for p in range(pieces):
            source = volume.at[pl.ds(k * share, share), :, pl.ds(p * LANES, LANES)]
            target = pad.at[pl.ds(k * share + 1, share), pl.ds(pad_row(tile_rows, p, 0), tile_rows)]
            fetches.append(pltpu.make_async_copy(source, target, sems.at[k * pieces + p]))
    for copy in small + fetches:
        copy.start()
    for copy in small:
        copy.wait()
    for k, table in enumerate(knot_tables(knot_ref, colour_ref, total_planes)):
        tables_ref[k] = table
    for fetch in fetches:
        fetch.wait()
    stride = tile_rows + 2 * ROWS
    near, far = [pad_row(tile_rows, 0, 0) + (tile_rows - 1) * at for at in (1 - tile, tile)]
    for plane in range(planes):
        row_near[plane] = pad[plane + 1, pl.ds(near, pieces, stride=stride), :]
        row_far[plane] = pad[plane + 1, pl.ds(far, pieces, stride=stride), :]
    for p in range(pieces):
        rows = slice(pad_row(tile_rows, p, 0), pad_row(tile_rows, p, tile_rows))
        lanes = slice(p * LANES, (p + 1) * LANES)
        plane_near[0, :, lanes] = pad[1 + (planes - 1) * (1 - core), rows, :]
        plane_far[0, :, lanes] = pad[1 + (planes - 1) * core, rows, :]


def pad_row(tile_rows, piece, row):
    return piece * (tile_rows + 2 * ROWS) + ROWS + row


def add_halo(pad, plane_near, plane_far, row_near, row_far):
    _, tile_rows, columns = plane_near.shape
    planes, pieces, _ = row_near.shape
    (core,), (tile,) = low_bits("slab", 0), low_bits("tile", 0)
    for p in range(pieces):
        lanes = slice(p * LANES, (p + 1) * LANES)
        rows = slice(pad_row(tile_rows, p, 0), pad_row(tile_rows, p, tile_rows))
        pad[(planes + 1) * (1 - core), rows, :] = plane_near[0, :, lanes]
        pad[(planes + 1) * core, rows, :] = plane_far[0, :, lanes]
    first, stride = pad_row(tile_rows, 0, -1), tile_rows + 2 * ROWS
    for plane in range(planes):
        pad[plane + 1, pl.ds(first + (tile_rows + 1) * (1 - tile), pieces, stride=stride), :] = row_near[plane]
        pad[plane + 1, pl.ds(first + (tile_rows + 1) * tile, pieces, stride=stride), :] = row_far[plane]


class Marcher:
    def __init__(self, pad, tables_ref, side_ref):
        self.pad = pad
        self.pieces = side_ref.shape[1] // LANES
        self.planes = pad.shape[0] - 2
        self.tables = [tables_ref[k] for k in range(tables_ref.shape[0])]
        at = self.tables[0]
        self.edges = [jnp.broadcast_to(at[k : k + 1], (ROWS, LANES)) for k in range(KNOTS)]
        self.lane = lax.broadcasted_iota(jnp.int32, (ROWS, LANES), 1)
        self.lanes = [slice(p * LANES, (p + 1) * LANES) for p in range(self.pieces)]
        sides = [jnp.broadcast_to(side_ref[:, c], (ROWS, LANES)) for c in self.lanes]
        self.toward = [side == 1 for side in sides]
        self.away = [side != 1 for side in sides]

    def read(self, group, plane, piece, shift=0):
        row = pad_row(ROWS * ROWS, piece, group + shift)
        return self.pad[plane + 1, pl.ds(row, ROWS, stride=ROWS), :]

    def start(self):
        zero = jnp.zeros((ROWS, LANES), jnp.float32)
        return [[zero] * self.pieces for _ in range(3)] + [[zero + 1.0] * self.pieces]

    def load(self, ref):
        return [[ref[k, :, c] for c in self.lanes] for k in range(4)]

    def store(self, ref, state):
        for k in range(4):
            for p, c in enumerate(self.lanes):
                ref[k, :, c] = state[k][p]

    def steps(self, state, group, planes, onward):
        held = {}
        for plane in planes:
            held = {
                q: held[q] if q in held else [self.read(group, q, p) for p in range(self.pieces)]
                for q in range(plane - 1, plane + 2)
            }
            state = self.step(state, group, plane, onward, *[held[plane + d] for d in (-1, 0, 1)])
        return state

    def step(self, state, group, plane, onward, before, here, after):
        lane, zero = self.lane, jnp.zeros((ROWS, LANES), jnp.float32)
        to_left = [pltpu.roll(v, LANES - 1, 1) for v in here] + [zero]
        to_right = [zero] + [pltpu.roll(v, 1, 1) for v in here]
        new = [[], [], [], []]
        for p, x in enumerate(here):
            depth = after[p] - before[p]
            rows = self.read(group, plane, p, 1) - self.read(group, plane, p, -1)
            col_up = jnp.where(lane == 0, to_right[p], to_right[p + 1])
            col_down = jnp.where(lane == LANES - 1, to_left[p + 1], to_left[p])
            across = col_down - col_up
            facing = jnp.abs(0.448 * depth + 0.42 * rows + 0.336 * across)
            square = depth * depth + rows * rows + (across * across + 4.0)
            shading = 0.3 + facing * lax.rsqrt(square)
            clipped = jnp.minimum(jnp.maximum(x, -3.0), 3.0)
            red, green, blue, exponent = look_up(clipped, self.tables, self.edges)
            passed = jnp.exp2(exponent)
            fade = jnp.where(onward[p], 1.0, passed)
            weight = jnp.where(onward[p], state[3][p], 1.0) * ((1.0 - passed) * shading)
            for channel, value in enumerate((red, green, blue)):
                new[channel].append(state[channel][p] * fade + weight * value)
            new[3].append(state[3][p] * passed)
        return new


def inner_kernel(pad, tables_ref, side_ref, states):
    marcher = Marcher(pad, tables_ref, side_ref)

    def group(j, carry):
        state = marcher.steps(marcher.start(), 1 + j, range(1, marcher.planes - 1), marcher.toward)
        marcher.store(states.at[1 + j], state)
        return carry

    lax.fori_loop(0, ROWS - 2, group, 0, unroll=INNER_UNROLL)


def finish(pad, states, tables_ref, side_ref, out, parity):
    marcher = Marcher(pad, tables_ref, side_ref)
    outermost = parity * (ROWS - 1)
    state = marcher.start()
    state = marcher.steps(state, outermost, range(marcher.planes), marcher.toward)
    marcher.store(out.at[parity * (ROWS // 2 - 1)], state)

    def group(j, carry):
        g = 2 - parity + 2 * j
        state = marcher.load(states.at[g])
        state = marcher.steps(state, g, [marcher.planes - 1], marcher.toward)
        state = marcher.steps(state, g, [0], marcher.away)
        marcher.store(out.at[1 - parity + j], state)
        return carry

    lax.fori_loop(0, ROWS // 2 - 1, group, 0, unroll=True)


def merge(first_is_front, mine, other):
    lead = jnp.where(first_is_front, mine[3], other[3])
    merged = [
        jnp.where(first_is_front, mine[c], other[c]) + lead * jnp.where(first_is_front, other[c], mine[c])
        for c in range(3)
    ]
    return merged + [mine[3] * other[3]]


def both_halves(value):
    sublane = lax.broadcasted_iota(jnp.int32, value.shape, 0)
    return jnp.where(sublane < 4, pltpu.roll(value, 4, 0), value)


def final_kernel(parts, side_ref, out):
    toward = jnp.concatenate([side_ref[...]] * 2, axis=0) == 1
    lower = lax.broadcasted_iota(jnp.int32, (ROWS, LANES), 0) < 4
    top = bottom = jnp.zeros((ROWS, LANES), jnp.float32)
    passing = jnp.ones((ROWS, LANES), jnp.float32)
    for k in range(parts.shape[0]):
        passed = both_halves(parts[k, ROWS:])
        fade = jnp.where(toward, 1.0, passed)
        weight = jnp.where(toward, passing, 1.0)
        top = top * fade + parts[k, :ROWS] * weight
        bottom = bottom * fade + parts[k, ROWS:] * weight
        passing = passing * passed
    out[:ROWS] = top
    out[ROWS:] = jnp.where(lower, bottom, 1.0 - passing)


def per_device(volume, knot_bins, colour_table, view_side):
    planes, tile_rows, columns = volume.shape
    slabs, tiles = lax.axis_size("slab"), lax.axis_size("tile")
    pieces = columns // LANES
    unit = 4 * pieces
    groups = ROWS // 2

    vmem = pl.BlockSpec(memory_space=pltpu.VMEM)
    hbm = pl.BlockSpec(memory_space=pltpu.HBM)
    small = pltpu.CompilerParams(vmem_limit_bytes=SMALL_VMEM)

    def array(*shape):
        return jax.ShapeDtypeStruct(shape, jnp.float32)

    inputs = (volume, knot_bins, colour_table, view_side.reshape(1, columns))
    inputs = [pltpu.with_memory_space_constraint(x, pltpu.HBM) for x in inputs]
    plane = pltpu.VMEM((1, tile_rows, columns), jnp.float32)
    row = pltpu.VMEM((planes, pieces, LANES), jnp.float32)
    pad, *edges, tables, side = pl.pallas_call(
        lambda *refs: load_kernel(planes * slabs, *refs),
        out_shape=[
            pltpu.VMEM((planes + 2, pieces * (tile_rows + 2 * ROWS), LANES), jnp.float32),
            plane, plane, row, row,
            pltpu.VMEM((9, ROWS, LANES), jnp.float32),
            pltpu.VMEM((1, columns), jnp.int32),
        ],
        in_specs=[hbm] * 4,
        out_specs=[vmem] * 7,
        scratch_shapes=[
            pltpu.SMEM((KNOTS,), jnp.int32),
            pltpu.SMEM((4, KNOTS), jnp.float32),
            pltpu.SemaphoreType.DMA((LOAD_PARTS * pieces,)),
            pltpu.SemaphoreType.DMA((3,)),
        ],
        compiler_params=small,
        name="load",
    )(*inputs)

    def swap(block, axis, size, low):
        route = [(i, i + 1) for i in range(low, size - 1, 2)]
        return lax.ppermute(block, axis, route + [(j, i) for i, j in route])

    halo = [
        swap(edges[0], "slab", slabs, 0),
        swap(edges[1], "slab", slabs, 1),
        swap(edges[2], "tile", tiles, 0),
        swap(edges[3], "tile", tiles, 1),
    ]

    def cost(steps):
        count = steps * ROWS * columns
        return pl.CostEstimate(flops=100 * count, bytes_accessed=16 * count, transcendentals=2 * count)

    inner = (ROWS - 2) * (planes - 2)
    outer = (ROWS * planes - inner) // 2
    states = pl.pallas_call(
        inner_kernel,
        out_shape=array(ROWS, 4, ROWS, columns),
        in_specs=[vmem] * 3,
        out_specs=vmem,
        compiler_params=small,
        cost_estimate=cost(inner),
        name="inner",
    )(pad, tables, side)

    def finish_sent(pad_in, near, far, row_near, row_far, states, tables, side, pad, out):
        add_halo(pad, near, far, row_near, row_far)
        (core,) = low_bits("slab", 0)
        finish(pad, states, tables, side, out, 1 - core)

    def finish_kept(pad, states, tables, side, out):
        (core,) = low_bits("slab", 0)
        finish(pad, states, tables, side, out, core)

    half = array(groups, 4, ROWS, columns)
    pad, sent = pl.pallas_call(
        finish_sent,
        out_shape=[array(*pad.shape), half],
        in_specs=[vmem] * 8,
        out_specs=[vmem] * 2,
        input_output_aliases={0: 0},
        compiler_params=small,
        cost_estimate=cost(outer),
        name="finish_sent",
    )(pad, *halo, states, tables, side)
    got = lax.ppermute(sent, "slab", [(i, i ^ 1) for i in range(slabs)])
    kept = pl.pallas_call(
        finish_kept,
        out_shape=half,
        in_specs=[vmem] * 4,
        out_specs=vmem,
        compiler_params=small,
        cost_estimate=cost(outer),
        name="finish_kept",
    )(pad, states, tables, side)

    def pair(mine, other, side_ref, out):
        (core,) = low_bits("slab", 0)
        for p in range(pieces):
            c = slice(p * LANES, (p + 1) * LANES)
            front = jnp.broadcast_to(side_ref[:, c], (ROWS, LANES)) + core == 1
            for x in range(groups):
                whole = merge(front, [mine[x, k, :, c] for k in range(4)], [other[x, k, :, c] for k in range(4)])
                for k, value in enumerate(whole):
                    out[pl.ds(x * unit + k * pieces + p, ROWS, stride=groups * unit), :] = value

    merged = pl.pallas_call(
        pair,
        out_shape=array(ROWS * groups * unit, LANES),
        in_specs=[vmem] * 3,
        out_specs=vmem,
        compiler_params=small,
        name="pair",
    )(kept, got, side)
    members = [[2 * q + c for q in range(slabs // 2)] for c in range(2)]
    parts = lax.all_to_all(
        merged.reshape(slabs // 2, unit, LANES), "slab", 0, 0, axis_index_groups=members, tiled=True
    )
    image = pl.pallas_call(
        final_kernel,
        out_shape=array(unit, LANES),
        in_specs=[vmem] * 2,
        out_specs=vmem,
        compiler_params=small,
        name="final",
    )(parts, side.reshape(pieces, LANES))
    return image.reshape(4, 1, 1, columns)


def solution(mesh):
    return jax.shard_map(
        per_device,
        mesh=mesh,
        in_specs=(P("slab", "tile", None), P(), P(), P()),
        out_specs=P(None, "slab", "tile", None),
        check_vma=False,
    )
```

time: 43.4 us -> 40.5 us (0.933); the launches traced: 42.7 us -> 40.4 us
  waiting for transfers between devices: 3.22 us -> 0.29 us
  starting transfers between devices: 6.05 us -> 7.98 us
  blocking collectives: 25.1 us -> 24.3 us
  Pallas kernels: 8.34 us -> 7.67 us
    ppermute x4, waiting for transfers between devices: 3.21 us -> 0.01 us  [swap(): return lax.ppermute(block, axis, route + [(j, i) for i, j in route])]
    ppermute x1, starting transfers between devices: 0.45 us -> 2.37 us  [per_device(): got = lax.ppermute(sent, 'slab', [(i, i ^ 1) for i in range(slabs)])]
    all_to_all x1, blocking collectives: 25.1 us -> 24.3 us  [per_device(): lax.all_to_all(merged.reshape(slabs // 2, unit, LANES), 'slab', 0, 0, axi...]
    pallas_call x1, Pallas kernels: 2.18 us -> 1.68 us  [per_device(): pl.pallas_call(lambda *refs: load_kernel(planes * slabs, *refs), out_shap...]
    pallas_call x2 -> x3, Pallas kernels: 5.32 us -> 5.15 us  [the longest x1 3.34 us: per_device(): pl.pallas_call(inner_kernel, out_shape=array(ROWS, 4, ROWS, columns), in_...]
  transfers between devices with their start and end apart: 5 -> 5, of which waited for: 1 -> 1; matrix products, arithmetic and copies ran while one was open for 0% -> 0% of each run, Pallas kernels for 6% -> 10%
where the time goes in v3:
time: 40.5 us; the launch traced here: 40.4 us
  blocking collectives  24.3 us (60%)
  starting transfers between devices  7.98 us (20%)
  Pallas kernels  7.67 us (19%)
    all_to_all x1, blocking collectives, per_device(): lax.all_to_all(merged.reshape(slabs // 2, unit, LANES), 'slab', 0, 0, axi...  24.3 us
    ppermute x4, starting transfers between devices, swap(): return lax.ppermute(block, axis, route + [(j, i) for i, j in route])  5.6 us
    pallas_call x1, Pallas kernels, per_device(): pl.pallas_call(inner_kernel, out_shape=array(ROWS, 4, ROWS, columns), in_...  3.34 us
    ppermute x1, starting transfers between devices, per_device(): got = lax.ppermute(sent, 'slab', [(i, i ^ 1) for i in range(slabs)])  2.37 us
    pallas_call x1, Pallas kernels, per_device(): pl.pallas_call(lambda *refs: load_kernel(planes * slabs, *refs), out_shap...  1.68 us
    pallas_call x1, Pallas kernels, per_device(): pl.pallas_call(finish_sent, out_shape=[array(*pad.shape), half], in_specs...  0.93 us
    pallas_call x1, Pallas kernels, per_device(): pl.pallas_call(finish_kept, out_shape=half, in_specs=[vmem] * 4, out_spec...  0.88 us
  transfers between devices with their start and end apart: 5, of which 1 were waited for; matrix products, arithmetic and copies ran while one was open for 0% of the time, Pallas kernels for 10%

profile of v3, /device:TPU:8, one launch (start us, length us, event | category | flops | bytes accessed | tf_op | source)
XLA Modules:
  0.0 40.4 jit_solution(15004690847245267651)
XLA Ops:
  0.0 1.7 %load.1 = (f32[18,320,128]{2,1,0:T(8,128)S(1)}, f32[1,64,512]{2,1,0:T(8,128)S(1)}, f32[1,64,512]{2,1,0:T(8,128)S(1)}, f32[16,4,128]{2,1,0:T(4,128)S(1)}, f32[16,...) custom-call(f32[16,64,512]{2,1,0:T(8,128)} %refs_0_.1, s32[8]{0:T(128)} %refs_1_.1, ...), custom_call_target="tpu_custom_call" | custom-call | tf_op jit(solution)/shard_map/load/pallas_call | solution.py:259
  1.7 0.1 collective-permute-start
  1.8 0.7 %collective-permute-start.1 = (f32[1,64,512]{2,1,0:T(8,128)S(1)}, f32[1,64,512]{2,1,0:T(8,128)S(1)}, u32[]{:S(2)}, u32[]{:S(2)}) collective-permute-start(f32[1,64,512]{2,1,0:T(8,128)S(1)} %get-tuple-element.16), channel_id=1, source_target_pairs={{4,8},{12,16},{20,24},{28,32},{36,40},{44,48},{52,56},{60,64},{68,... | collective-permute-start | bytes 393224 | tf_op jit(solution)/shard_map/ppermute | solution.py:281
  2.5 2.3 %collective-permute-start.2 = (f32[16,4,128]{2,1,0:T(4,128)S(1)}, f32[16,4,128]{2,1,0:T(4,128)S(1)}, u32[]{:S(2)}, u32[]{:S(2)}) collective-permute-start(f32[16,4,128]{2,1,0:T(4,128)S(1)} %get-tuple-element.17), channel_id=1, source_target_pairs={{0,1},{2,3},{1,0},{3,2},{4,5},{6,7},{5,4},{7,6},{8,9},{10,11},{9,8... | collective-permute-start | bytes 98312 | tf_op jit(solution)/shard_map/ppermute | solution.py:281
  4.7 2.6 %collective-permute-start.3 = (f32[16,4,128]{2,1,0:T(4,128)S(1)}, f32[16,4,128]{2,1,0:T(4,128)S(1)}, u32[]{:S(2)}, u32[]{:S(2)}) collective-permute-start(f32[16,4,128]{2,1,0:T(4,128)S(1)} %get-tuple-element.18), channel_id=1, source_target_pairs={{1,2},{2,1},{5,6},{6,5},{9,10},{10,9},{13,14},{14,13},{17,18},{18,... | collective-permute-start | bytes 98312 | tf_op jit(solution)/shard_map/ppermute | solution.py:281
  7.3 3.3 %inner.1.states = f32[8,4,8,512]{3,2,1,0:T(8,128)S(1)} custom-call(f32[18,320,128]{2,1,0:T(8,128)S(1)} %get-tuple-element.14.pad.pad_in, f32[9,8,128]{2,1,0:T(8,128)S(1)} %get-tuple-element.19.tables_ref.tables, s32[1,512]{1,0:T(1,128)S(1)} %get-tuple-element.20.side_ref.side), custom_call_target="tpu_custom_call" | custom-call | flops 34406400 | bytes 5505024 | tf_op jit(solution)/shard_map/inner/pallas_call | solution.py:296
  10.7 0.0 collective-permute-done.2.row_near
  10.7 0.0 collective-permute-done.3.row_far
  10.7 0.0 collective-permute-done.near
  10.7 0.0 collective-permute-done.1.far
  10.7 0.9 %finish_sent.1 = (f32[18,320,128]{2,1,0:T(8,128)S(1)}, f32[4,4,8,512]{3,2,1,0:T(8,128)S(1)}) custom-call(f32[18,320,128]{2,1,0:T(8,128)S(1)} %get-tuple-element.14.pad.pad_in, f32[1,64,512]{2,1,0:T(8,128)S(1)} %collective-permute-done.near, f32[1,64,512]{2,1,0:T(8,128)S(1)} %collective-permute-done.1.far, ...), custom_call_target="tpu_custom_call", output_to_operand_aliasing={{0}: (0, {})} | custom-call | flops 9011200 | bytes 1441792 | tf_op jit(solution)/shard_map/finish_sent/pallas_call | solution.py:316
  11.6 2.4 %collective-permute-start.4 = (f32[4,4,8,512]{3,2,1,0:T(8,128)S(1)}, f32[4,4,8,512]{3,2,1,0:T(8,128)S(1)}, u32[]{:S(2)}, u32[]{:S(2)}) collective-permute-start(f32[4,4,8,512]{3,2,1,0:T(8,128)S(1)} %get-tuple-element.22), channel_id=1, source_target_pairs={{0,4},{4,0},{8,12},{12,8},{16,20},{20,16},{24,28},{28,24},{32,36},... | collective-permute-start | bytes 786440 | tf_op jit(solution)/shard_map/ppermute | solution.py:326
  14.0 0.9 %finish_kept.1.mine = f32[4,4,8,512]{3,2,1,0:T(8,128)S(1)} custom-call(f32[18,320,128]{2,1,0:T(8,128)S(1)} %get-tuple-element.21.pad, f32[8,4,8,512]{3,2,1,0:T(8,128)S(1)} %inner.1.states, f32[9,8,128]{2,1,0:T(8,128)S(1)} %get-tuple-element.19.tables_ref.tables, s32[1,512]{1,0:T(1,128)S(1)} %get-tuple-element.20.side_ref.side), custom_call_target="tpu_custom_call" | custom-call | flops 9011200 | bytes 1441792 | tf_op jit(solution)/shard_map/finish_kept/pallas_call | solution.py:327
  14.9 0.3 collective-permute-done.4.other
  15.2 0.2 pair.1
  15.4 24.3 %all_to_all.5.parts = f32[32,16,128]{2,1,0:T(8,128)S(1)} all-to-all(f32[32,16,128]{2,1,0:T(8,128)S(1)} %bitcast.4), channel_id=1, replica_groups={{0,8,16,24,32,40,48,56,64,72,80,88,96,104,112,120,128,136,144,152,160,1..., dimensions={0} | all-to-all | bytes 524288 | tf_op jit(solution)/shard_map/all_to_all | solution.py:356
  39.7 0.7 %final.1 = f32[16,128]{1,0:T(8,128)} custom-call(f32[32,16,128]{2,1,0:T(8,128)S(1)} %all_to_all.5.parts, s32[4,128]{1,0:T(4,128)S(1)} %bitcast.5), custom_call_target="tpu_custom_call" | custom-call | tf_op jit(solution)/shard_map/final/pallas_call | solution.py:359
Async XLA Ops:
  1.7 9.0 %collective-permute-start = (f32[1,64,512]{2,1,0:T(8,128)S(1)}, f32[1,64,512]{2,1,0:T(8,128)S(1)}, u32[]{:S(2)}, u32[]{:S(2)}) collective-permute-start(f32[1,64,512]{2,1,0:T(8,128)S(1)} %get-tuple-element.15), channel_id=1, source_target_pairs={{0,4},{8,12},{16,20},{24,28},{32,36},{40,44},{48,52},{56,60},{64,6... | collective-permute-start | bytes 393224 | tf_op jit(solution)/shard_map/ppermute | solution.py:281
  1.8 8.9 %collective-permute-start.1 = (f32[1,64,512]{2,1,0:T(8,128)S(1)}, f32[1,64,512]{2,1,0:T(8,128)S(1)}, u32[]{:S(2)}, u32[]{:S(2)}) collective-permute-start(f32[1,64,512]{2,1,0:T(8,128)S(1)} %get-tuple-element.16), channel_id=1, source_target_pairs={{4,8},{12,16},{20,24},{28,32},{36,40},{44,48},{52,56},{60,64},{68,... | collective-permute-start | bytes 393224 | tf_op jit(solution)/shard_map/ppermute | solution.py:281
  2.5 8.2 %collective-permute-start.2 = (f32[16,4,128]{2,1,0:T(4,128)S(1)}, f32[16,4,128]{2,1,0:T(4,128)S(1)}, u32[]{:S(2)}, u32[]{:S(2)}) collective-permute-start(f32[16,4,128]{2,1,0:T(4,128)S(1)} %get-tuple-element.17), channel_id=1, source_target_pairs={{0,1},{2,3},{1,0},{3,2},{4,5},{6,7},{5,4},{7,6},{8,9},{10,11},{9,8... | collective-permute-start | bytes 98312 | tf_op jit(solution)/shard_map/ppermute | solution.py:281
  4.7 5.9 %collective-permute-start.3 = (f32[16,4,128]{2,1,0:T(4,128)S(1)}, f32[16,4,128]{2,1,0:T(4,128)S(1)}, u32[]{:S(2)}, u32[]{:S(2)}) collective-permute-start(f32[16,4,128]{2,1,0:T(4,128)S(1)} %get-tuple-element.18), channel_id=1, source_target_pairs={{1,2},{2,1},{5,6},{6,5},{9,10},{10,9},{13,14},{14,13},{17,18},{18,... | collective-permute-start | bytes 98312 | tf_op jit(solution)/shard_map/ppermute | solution.py:281
  11.6 3.5 %collective-permute-start.4 = (f32[4,4,8,512]{3,2,1,0:T(8,128)S(1)}, f32[4,4,8,512]{3,2,1,0:T(8,128)S(1)}, u32[]{:S(2)}, u32[]{:S(2)}) collective-permute-start(f32[4,4,8,512]{3,2,1,0:T(8,128)S(1)} %get-tuple-element.22), channel_id=1, source_target_pairs={{0,4},{4,0},{8,12},{12,8},{16,20},{20,16},{24,28},{28,24},{32,36},... | collective-permute-start | bytes 786440 | tf_op jit(solution)/shard_map/ppermute | solution.py:326

commit v4 on v3

--- a/solution.py
+++ b/solution.py
@@ -11,8 +11,9 @@
 LANES = 128
 ROWS = 8
 SMALL_VMEM = 4 << 20
+FACING = 0.7 * 0.64
 LOAD_PARTS = 1
-INNER_UNROLL = 2
+INNER_UNROLL = 5
 
 
 def knot_tables(knot_bins, colour_table, total_planes):
@@ -33,7 +34,7 @@
         start = spread(lambda knot: colour_table[channel, knot])
         rise = (pltpu.roll(start, KNOTS - 1, 0) - start) / width
         slope = jnp.where(sublane == KNOTS - 1, 0.0, rise)
-        factor = -400.0 / total_planes * LOG2_E if channel == 3 else 1.0
+        factor = -400.0 / total_planes * LOG2_E if channel == 3 else FACING
         starts.append(start * factor)
         slopes.append(slope * factor)
     return [knot_at] + starts + slopes
@@ -115,8 +116,8 @@
 
 
 class Marcher:
-    def __init__(self, pad, tables_ref, side_ref):
-        self.pad = pad
+    def __init__(self, pad, tables_ref, side_ref, stash):
+        self.pad, self.stash = pad, stash
         self.pieces = side_ref.shape[1] // LANES
         self.planes = pad.shape[0] - 2
         self.tables = [tables_ref[k] for k in range(tables_ref.shape[0])]
@@ -124,9 +125,7 @@
         self.edges = [jnp.broadcast_to(at[k : k + 1], (ROWS, LANES)) for k in range(KNOTS)]
         self.lane = lax.broadcasted_iota(jnp.int32, (ROWS, LANES), 1)
         self.lanes = [slice(p * LANES, (p + 1) * LANES) for p in range(self.pieces)]
-        sides = [jnp.broadcast_to(side_ref[:, c], (ROWS, LANES)) for c in self.lanes]
-        self.toward = [side == 1 for side in sides]
-        self.away = [side != 1 for side in sides]
+        self.toward = [jnp.broadcast_to(side_ref[:, c], (ROWS, LANES)) == 1 for c in self.lanes]
 
     def read(self, group, plane, piece, shift=0):
         row = pad_row(ROWS * ROWS, piece, group + shift)
@@ -144,68 +143,102 @@
             for p, c in enumerate(self.lanes):
                 ref[k, :, c] = state[k][p]
 
-    def steps(self, state, group, planes, onward):
-        held = {}
-        for plane in planes:
-            held = {
-                q: held[q] if q in held else [self.read(group, q, p) for p in range(self.pieces)]
-                for q in range(plane - 1, plane + 2)
-            }
-            state = self.step(state, group, plane, onward, *[held[plane + d] for d in (-1, 0, 1)])
-        return state
-
-    def step(self, state, group, plane, onward, before, here, after):
+    def shade(self, group, plane, held):
         lane, zero = self.lane, jnp.zeros((ROWS, LANES), jnp.float32)
+        for q in range(plane - 1, plane + 2):
+            if q not in held:
+                held[q] = [self.read(group, q, p) for p in range(self.pieces)]
+        before, here, after = [held[plane + d] for d in (-1, 0, 1)]
         to_left = [pltpu.roll(v, LANES - 1, 1) for v in here] + [zero]
         to_right = [zero] + [pltpu.roll(v, 1, 1) for v in here]
-        new = [[], [], [], []]
-        for p, x in enumerate(here):
+        strengths = []
+        for p in range(self.pieces):
             depth = after[p] - before[p]
             rows = self.read(group, plane, p, 1) - self.read(group, plane, p, -1)
             col_up = jnp.where(lane == 0, to_right[p], to_right[p + 1])
             col_down = jnp.where(lane == LANES - 1, to_left[p + 1], to_left[p])
             across = col_down - col_up
-            facing = jnp.abs(0.448 * depth + 0.42 * rows + 0.336 * across)
+            facing = jnp.abs(depth + (0.6 / 0.64) * rows + (0.48 / 0.64) * across)
             square = depth * depth + rows * rows + (across * across + 4.0)
-            shading = 0.3 + facing * lax.rsqrt(square)
+            strengths.append(0.3 / FACING + facing * lax.rsqrt(square))
+        return here, strengths
+
+    def pair(self, group, plane, held):
+        (low, low_strength), (high, high_strength) = [
+            self.shade(group, q, held) for q in (plane, self.planes - 1 - plane)
+        ]
+        near, far = [], []
+        for p, toward in enumerate(self.toward):
+            near.append((jnp.where(toward, low[p], high[p]), jnp.where(toward, low_strength[p], high_strength[p])))
+            far.append((jnp.where(toward, high[p], low[p]), jnp.where(toward, high_strength[p], low_strength[p])))
+        return near, far
+
+    def behind(self, state, plane):
+        new = [[], [], [], []]
+        for p, (x, strength) in enumerate(plane):
             clipped = jnp.minimum(jnp.maximum(x, -3.0), 3.0)
             red, green, blue, exponent = look_up(clipped, self.tables, self.edges)
-            passed = jnp.exp2(exponent)
-            fade = jnp.where(onward[p], 1.0, passed)
-            weight = jnp.where(onward[p], state[3][p], 1.0) * ((1.0 - passed) * shading)
+            left = state[3][p] * jnp.exp2(exponent)
+            weight = (state[3][p] - left) * strength
             for channel, value in enumerate((red, green, blue)):
-                new[channel].append(state[channel][p] * fade + weight * value)
-            new[3].append(state[3][p] * passed)
+                new[channel].append(state[channel][p] + weight * value)
+            new[3].append(left)
         return new
 
-
-def inner_kernel(pad, tables_ref, side_ref, states):
-    marcher = Marcher(pad, tables_ref, side_ref)
+    def run(self, group, first):
+        state, held = self.start(), {}
+        for plane in range(first, self.planes // 2):
+            near, far = self.pair(group, plane, held)
+            state = self.behind(state, near)
+            for p in range(self.pieces):
+                for k in range(2):
+                    self.stash[(plane * self.pieces + p) * 2 + k] = far[p][k]
+        for plane in reversed(range(first, self.planes // 2)):
+            at = [(plane * self.pieces + p) * 2 for p in range(self.pieces)]
+            state = self.behind(state, [(self.stash[k], self.stash[k + 1]) for k in at])
+        return state
+
+    def ends(self, state, group):
+        near, far = self.pair(group, 0, {})
+        front = self.behind(self.start(), near)
+        state = [
+            [front[k][p] + front[3][p] * state[k][p] if k < 3 else front[3][p] * state[3][p] for p in range(self.pieces)]
+            for k in range(4)
+        ]
+        return self.behind(state, far)
+
+
+def late_group(parity):
+    return ROWS - 2 - parity
+
+
+def inner_kernel(pad, tables_ref, side_ref, states, stash):
+    marcher = Marcher(pad, tables_ref, side_ref, stash)
+    (core,) = low_bits("slab", 0)
 
     def group(j, carry):
-        state = marcher.steps(marcher.start(), 1 + j, range(1, marcher.planes - 1), marcher.toward)
-        marcher.store(states.at[1 + j], state)
+        g = 1 + j + (1 + j >= late_group(core)).astype(jnp.int32)
+        marcher.store(states.at[g], marcher.run(g, 1))
         return carry
 
-    lax.fori_loop(0, ROWS - 2, group, 0, unroll=INNER_UNROLL)
-
-
-def finish(pad, states, tables_ref, side_ref, out, parity):
-    marcher = Marcher(pad, tables_ref, side_ref)
-    outermost = parity * (ROWS - 1)
-    state = marcher.start()
-    state = marcher.steps(state, outermost, range(marcher.planes), marcher.toward)
-    marcher.store(out.at[parity * (ROWS // 2 - 1)], state)
+    lax.fori_loop(0, ROWS - 3, group, 0, unroll=INNER_UNROLL)
+
+
+def finish(pad, states, tables_ref, side_ref, out, stash, parity, left):
+    marcher = Marcher(pad, tables_ref, side_ref, stash)
+
+    def whole(t, carry):
+        g = jnp.where(t == 0, parity * (ROWS - 1), late_group(parity))
+        marcher.store(out.at[g >> 1], marcher.run(g, 0))
+        return carry
 
     def group(j, carry):
         g = 2 - parity + 2 * j
-        state = marcher.load(states.at[g])
-        state = marcher.steps(state, g, [marcher.planes - 1], marcher.toward)
-        state = marcher.steps(state, g, [0], marcher.away)
-        marcher.store(out.at[1 - parity + j], state)
+        marcher.store(out.at[g >> 1], marcher.ends(marcher.load(states.at[g]), g))
         return carry
 
-    lax.fori_loop(0, ROWS // 2 - 1, group, 0, unroll=True)
+    lax.fori_loop(0, left, whole, 0, unroll=True)
+    lax.fori_loop(0, ROWS // 2 - left, group, 0, unroll=True)
 
 
 def merge(first_is_front, mine, other):
@@ -225,15 +258,18 @@
 def final_kernel(parts, side_ref, out):
     toward = jnp.concatenate([side_ref[...]] * 2, axis=0) == 1
     lower = lax.broadcasted_iota(jnp.int32, (ROWS, LANES), 0) < 4
-    top = bottom = jnp.zeros((ROWS, LANES), jnp.float32)
-    passing = jnp.ones((ROWS, LANES), jnp.float32)
-    for k in range(parts.shape[0]):
-        passed = both_halves(parts[k, ROWS:])
-        fade = jnp.where(toward, 1.0, passed)
-        weight = jnp.where(toward, passing, 1.0)
-        top = top * fade + parts[k, :ROWS] * weight
-        bottom = bottom * fade + parts[k, ROWS:] * weight
-        passing = passing * passed
+    whole = [(parts[k, :ROWS], parts[k, ROWS:], both_halves(parts[k, ROWS:])) for k in range(parts.shape[0])]
+    while len(whole) > 1:
+        joined = []
+        for (top, bottom, passing), (top_2, bottom_2, passing_2) in zip(whole[::2], whole[1::2]):
+            lead = jnp.where(toward, passing, passing_2)
+            joined.append((
+                jnp.where(toward, top, top_2) + lead * jnp.where(toward, top_2, top),
+                jnp.where(toward, bottom, bottom_2) + lead * jnp.where(toward, bottom_2, bottom),
+                passing * passing_2,
+            ))
+        whole = joined
+    top, bottom, passing = whole[0]
     out[:ROWS] = top
     out[ROWS:] = jnp.where(lower, bottom, 1.0 - passing)
 
@@ -291,26 +327,28 @@
         count = steps * ROWS * columns
         return pl.CostEstimate(flops=100 * count, bytes_accessed=16 * count, transcendentals=2 * count)
 
-    inner = (ROWS - 2) * (planes - 2)
+    inner = (ROWS - 3) * (planes - 2)
     outer = (ROWS * planes - inner) // 2
+    stash = pltpu.VMEM((planes * pieces, ROWS, LANES), jnp.float32)
     states = pl.pallas_call(
         inner_kernel,
         out_shape=array(ROWS, 4, ROWS, columns),
         in_specs=[vmem] * 3,
         out_specs=vmem,
+        scratch_shapes=[stash],
         compiler_params=small,
         cost_estimate=cost(inner),
         name="inner",
     )(pad, tables, side)
 
-    def finish_sent(pad_in, near, far, row_near, row_far, states, tables, side, pad, out):
+    def finish_sent(pad_in, near, far, row_near, row_far, states, tables, side, pad, out, stash):
         add_halo(pad, near, far, row_near, row_far)
         (core,) = low_bits("slab", 0)
-        finish(pad, states, tables, side, out, 1 - core)
-
-    def finish_kept(pad, states, tables, side, out):
+        finish(pad, states, tables, side, out, stash, 1 - core, 1)
+
+    def finish_kept(pad, states, tables, side, out, stash):
         (core,) = low_bits("slab", 0)
-        finish(pad, states, tables, side, out, core)
+        finish(pad, states, tables, side, out, stash, core, 2)
 
     half = array(groups, 4, ROWS, columns)
     pad, sent = pl.pallas_call(
@@ -319,6 +357,7 @@
         in_specs=[vmem] * 8,
         out_specs=[vmem] * 2,
         input_output_aliases={0: 0},
+        scratch_shapes=[stash],
         compiler_params=small,
         cost_estimate=cost(outer),
         name="finish_sent",
@@ -329,6 +368,7 @@
         out_shape=half,
         in_specs=[vmem] * 4,
         out_specs=vmem,
+        scratch_shapes=[stash],
         compiler_params=small,
         cost_estimate=cost(outer),
         name="finish_kept",

time: 40.5 us -> 40.1 us (level)
  starting transfers between devices: 7.98 us -> 7.45 us
    pallas_call x1, Pallas kernels: 3.34 us -> 2.64 us  [per_device(): pl.pallas_call(inner_kernel, out_shape=array(ROWS, 4, ROWS, columns), in_...]
    ppermute x4, waiting for transfers between devices: 0.01 us -> 0.57 us  [swap(): return lax.ppermute(block, axis, route + [(j, i) for i, j in route])]
    ppermute x1, starting transfers between devices: 2.37 us -> 1.84 us  [per_device(): got = lax.ppermute(sent, 'slab', [(i, i ^ 1) for i in range(slabs)])]
    pallas_call x1, Pallas kernels: 0.88 us -> 1.4 us  [per_device(): pl.pallas_call(finish_kept, out_shape=half, in_specs=[vmem] * 4, out_spec...]
where the time goes in v4:
time: 40.1 us; the launch traced here: 39.9 us
  blocking collectives  24.4 us (61%)
  starting transfers between devices  7.45 us (19%)
  Pallas kernels  7.43 us (19%)
  waiting for transfers between devices  0.57 us (1%)
    all_to_all x1, blocking collectives, per_device(): lax.all_to_all(merged.reshape(slabs // 2, unit, LANES), 'slab', 0, 0, axi...  24.4 us
    ppermute x4, starting transfers between devices, swap(): return lax.ppermute(block, axis, route + [(j, i) for i, j in route])  5.6 us
    pallas_call x1, Pallas kernels, per_device(): pl.pallas_call(inner_kernel, out_shape=array(ROWS, 4, ROWS, columns), in_...  2.64 us
    ppermute x1, starting transfers between devices, per_device(): got = lax.ppermute(sent, 'slab', [(i, i ^ 1) for i in range(slabs)])  1.84 us
    pallas_call x1, Pallas kernels, per_device(): pl.pallas_call(lambda *refs: load_kernel(planes * slabs, *refs), out_shap...  1.68 us
    pallas_call x1, Pallas kernels, per_device(): pl.pallas_call(finish_kept, out_shape=half, in_specs=[vmem] * 4, out_spec...  1.4 us
    pallas_call x1, Pallas kernels, per_device(): pl.pallas_call(finish_sent, out_shape=[array(*pad.shape), half], in_specs...  0.88 us
  transfers between devices with their start and end apart: 5, of which 1 were waited for; matrix products, arithmetic and copies ran while one was open for 0% of the time, Pallas kernels for 10%

profile of v4, /device:TPU:8, one launch (start us, length us, event | category | flops | bytes accessed | tf_op | source)
XLA Modules:
  0.0 39.9 jit_solution(4157433059583607355)
XLA Ops:
  0.0 1.7 %load.1 = (f32[18,320,128]{2,1,0:T(8,128)S(1)}, f32[1,64,512]{2,1,0:T(8,128)S(1)}, f32[1,64,512]{2,1,0:T(8,128)S(1)}, f32[16,4,128]{2,1,0:T(4,128)S(1)}, f32[16,...) custom-call(f32[16,64,512]{2,1,0:T(8,128)} %refs_0_.1, s32[8]{0:T(128)} %refs_1_.1, ...), custom_call_target="tpu_custom_call" | custom-call | tf_op jit(solution)/shard_map/load/pallas_call | solution.py:295
  1.7 0.1 collective-permute-start
  1.8 0.7 %collective-permute-start.1 = (f32[1,64,512]{2,1,0:T(8,128)S(1)}, f32[1,64,512]{2,1,0:T(8,128)S(1)}, u32[]{:S(2)}, u32[]{:S(2)}) collective-permute-start(f32[1,64,512]{2,1,0:T(8,128)S(1)} %get-tuple-element.16), channel_id=1, source_target_pairs={{4,8},{12,16},{20,24},{28,32},{36,40},{44,48},{52,56},{60,64},{68,... | collective-permute-start | bytes 393224 | tf_op jit(solution)/shard_map/ppermute | solution.py:317
  2.5 2.3 %collective-permute-start.2 = (f32[16,4,128]{2,1,0:T(4,128)S(1)}, f32[16,4,128]{2,1,0:T(4,128)S(1)}, u32[]{:S(2)}, u32[]{:S(2)}) collective-permute-start(f32[16,4,128]{2,1,0:T(4,128)S(1)} %get-tuple-element.17), channel_id=1, source_target_pairs={{0,1},{2,3},{1,0},{3,2},{4,5},{6,7},{5,4},{7,6},{8,9},{10,11},{9,8... | collective-permute-start | bytes 98312 | tf_op jit(solution)/shard_map/ppermute | solution.py:317
  4.7 2.6 %collective-permute-start.3 = (f32[16,4,128]{2,1,0:T(4,128)S(1)}, f32[16,4,128]{2,1,0:T(4,128)S(1)}, u32[]{:S(2)}, u32[]{:S(2)}) collective-permute-start(f32[16,4,128]{2,1,0:T(4,128)S(1)} %get-tuple-element.18), channel_id=1, source_target_pairs={{1,2},{2,1},{5,6},{6,5},{9,10},{10,9},{13,14},{14,13},{17,18},{18,... | collective-permute-start | bytes 98312 | tf_op jit(solution)/shard_map/ppermute | solution.py:317
  7.3 2.6 %inner.1.states = f32[8,4,8,512]{3,2,1,0:T(8,128)S(1)} custom-call(f32[18,320,128]{2,1,0:T(8,128)S(1)} %get-tuple-element.14.pad.pad_in, f32[9,8,128]{2,1,0:T(8,128)S(1)} %get-tuple-element.19.tables_ref.tables, s32[1,512]{1,0:T(1,128)S(1)} %get-tuple-element.20.side_ref.side), custom_call_target="tpu_custom_call" | custom-call | flops 28672000 | bytes 4587520 | tf_op jit(solution)/shard_map/inner/pallas_call | solution.py:333
  10.0 0.0 collective-permute-done.2.row_near
  10.0 0.6 %collective-permute-done.3.row_far = f32[16,4,128]{2,1,0:T(4,128)S(1)} collective-permute-done((f32[16,4,128]{2,1,0:T(4,128)S(1)}, f32[16,4,128]{2,1,0:T(4,128)S(1)}, u32[]{:S(2)}, u32[]{:S(2)}) %collective-permute-start.3) | collective-permute-done | bytes 32800 | tf_op jit(solution)/shard_map/ppermute | solution.py:317
  10.5 0.0 collective-permute-done.near
  10.5 0.0 collective-permute-done.1.far
  10.5 0.9 %finish_sent.1 = (f32[18,320,128]{2,1,0:T(8,128)S(1)}, f32[4,4,8,512]{3,2,1,0:T(8,128)S(1)}) custom-call(f32[18,320,128]{2,1,0:T(8,128)S(1)} %get-tuple-element.14.pad.pad_in, f32[1,64,512]{2,1,0:T(8,128)S(1)} %collective-permute-done.near, f32[1,64,512]{2,1,0:T(8,128)S(1)} %collective-permute-done.1.far, ...), custom_call_target="tpu_custom_call", output_to_operand_aliasing={{0}: (0, {})} | custom-call | flops 11878400 | bytes 1900544 | tf_op jit(solution)/shard_map/finish_sent/pallas_call | solution.py:354
  11.4 1.8 %collective-permute-start.4 = (f32[4,4,8,512]{3,2,1,0:T(8,128)S(1)}, f32[4,4,8,512]{3,2,1,0:T(8,128)S(1)}, u32[]{:S(2)}, u32[]{:S(2)}) collective-permute-start(f32[4,4,8,512]{3,2,1,0:T(8,128)S(1)} %get-tuple-element.22), channel_id=1, source_target_pairs={{0,4},{4,0},{8,12},{12,8},{16,20},{20,16},{24,28},{28,24},{32,36},... | collective-permute-start | bytes 786440 | tf_op jit(solution)/shard_map/ppermute | solution.py:365
  13.3 1.4 %finish_kept.1.mine = f32[4,4,8,512]{3,2,1,0:T(8,128)S(1)} custom-call(f32[18,320,128]{2,1,0:T(8,128)S(1)} %get-tuple-element.21.pad, f32[8,4,8,512]{3,2,1,0:T(8,128)S(1)} %inner.1.states, f32[9,8,128]{2,1,0:T(8,128)S(1)} %get-tuple-element.19.tables_ref.tables, s32[1,512]{1,0:T(1,128)S(1)} %get-tuple-element.20.side_ref.side), custom_call_target="tpu_custom_call" | custom-call | flops 11878400 | bytes 1900544 | tf_op jit(solution)/shard_map/finish_kept/pallas_call | solution.py:366
  14.7 0.0 collective-permute-done.4.other
  14.7 0.2 pair.1
  14.9 24.4 %all_to_all.5.parts = f32[32,16,128]{2,1,0:T(8,128)S(1)} all-to-all(f32[32,16,128]{2,1,0:T(8,128)S(1)} %bitcast.4), channel_id=1, replica_groups={{0,8,16,24,32,40,48,56,64,72,80,88,96,104,112,120,128,136,144,152,160,1..., dimensions={0} | all-to-all | bytes 524288 | tf_op jit(solution)/shard_map/all_to_all | solution.py:396
  39.3 0.7 %final.1 = f32[16,128]{1,0:T(8,128)} custom-call(f32[32,16,128]{2,1,0:T(8,128)S(1)} %all_to_all.5.parts, s32[4,128]{1,0:T(4,128)S(1)} %bitcast.5), custom_call_target="tpu_custom_call" | custom-call | tf_op jit(solution)/shard_map/final/pallas_call | solution.py:399
Async XLA Ops:
  1.7 8.8 %collective-permute-start = (f32[1,64,512]{2,1,0:T(8,128)S(1)}, f32[1,64,512]{2,1,0:T(8,128)S(1)}, u32[]{:S(2)}, u32[]{:S(2)}) collective-permute-start(f32[1,64,512]{2,1,0:T(8,128)S(1)} %get-tuple-element.15), channel_id=1, source_target_pairs={{0,4},{8,12},{16,20},{24,28},{32,36},{40,44},{48,52},{56,60},{64,6... | collective-permute-start | bytes 393224 | tf_op jit(solution)/shard_map/ppermute | solution.py:317
  1.8 8.8 %collective-permute-start.1 = (f32[1,64,512]{2,1,0:T(8,128)S(1)}, f32[1,64,512]{2,1,0:T(8,128)S(1)}, u32[]{:S(2)}, u32[]{:S(2)}) collective-permute-start(f32[1,64,512]{2,1,0:T(8,128)S(1)} %get-tuple-element.16), channel_id=1, source_target_pairs={{4,8},{12,16},{20,24},{28,32},{36,40},{44,48},{52,56},{60,64},{68,... | collective-permute-start | bytes 393224 | tf_op jit(solution)/shard_map/ppermute | solution.py:317
  2.5 7.5 %collective-permute-start.2 = (f32[16,4,128]{2,1,0:T(4,128)S(1)}, f32[16,4,128]{2,1,0:T(4,128)S(1)}, u32[]{:S(2)}, u32[]{:S(2)}) collective-permute-start(f32[16,4,128]{2,1,0:T(4,128)S(1)} %get-tuple-element.17), channel_id=1, source_target_pairs={{0,1},{2,3},{1,0},{3,2},{4,5},{6,7},{5,4},{7,6},{8,9},{10,11},{9,8... | collective-permute-start | bytes 98312 | tf_op jit(solution)/shard_map/ppermute | solution.py:317
  4.7 5.8 %collective-permute-start.3 = (f32[16,4,128]{2,1,0:T(4,128)S(1)}, f32[16,4,128]{2,1,0:T(4,128)S(1)}, u32[]{:S(2)}, u32[]{:S(2)}) collective-permute-start(f32[16,4,128]{2,1,0:T(4,128)S(1)} %get-tuple-element.18), channel_id=1, source_target_pairs={{1,2},{2,1},{5,6},{6,5},{9,10},{10,9},{13,14},{14,13},{17,18},{18,... | collective-permute-start | bytes 98312 | tf_op jit(solution)/shard_map/ppermute | solution.py:317
  11.4 3.3 %collective-permute-start.4 = (f32[4,4,8,512]{3,2,1,0:T(8,128)S(1)}, f32[4,4,8,512]{3,2,1,0:T(8,128)S(1)}, u32[]{:S(2)}, u32[]{:S(2)}) collective-permute-start(f32[4,4,8,512]{3,2,1,0:T(8,128)S(1)} %get-tuple-element.22), channel_id=1, source_target_pairs={{0,4},{4,0},{8,12},{12,8},{16,20},{20,16},{24,28},{28,24},{32,36},... | collective-permute-start | bytes 786440 | tf_op jit(solution)/shard_map/ppermute | solution.py:365

commit v5 on v4

--- a/solution.py
+++ b/solution.py
@@ -100,6 +100,11 @@
     return piece * (tile_rows + 2 * ROWS) + ROWS + row
 
 
+def at_end(axis):
+    index = lax.axis_index(axis)
+    return (index == 0) | (index == lax.axis_size(axis) - 1)
+
+
 def add_halo(pad, plane_near, plane_far, row_near, row_far):
     _, tile_rows, columns = plane_near.shape
     planes, pieces, _ = row_near.shape
@@ -108,11 +113,12 @@
         lanes = slice(p * LANES, (p + 1) * LANES)
         rows = slice(pad_row(tile_rows, p, 0), pad_row(tile_rows, p, tile_rows))
         pad[(planes + 1) * (1 - core), rows, :] = plane_near[0, :, lanes]
-        pad[(planes + 1) * core, rows, :] = plane_far[0, :, lanes]
+        pad[(planes + 1) * core, rows, :] = jnp.where(at_end("slab"), 0.0, plane_far[0, :, lanes])
     first, stride = pad_row(tile_rows, 0, -1), tile_rows + 2 * ROWS
     for plane in range(planes):
         pad[plane + 1, pl.ds(first + (tile_rows + 1) * (1 - tile), pieces, stride=stride), :] = row_near[plane]
-        pad[plane + 1, pl.ds(first + (tile_rows + 1) * tile, pieces, stride=stride), :] = row_far[plane]
+        far = jnp.where(at_end("tile"), 0.0, row_far[plane])
+        pad[plane + 1, pl.ds(first + (tile_rows + 1) * tile, pieces, stride=stride), :] = far
 
 
 class Marcher:
@@ -313,7 +319,7 @@
     )(*inputs)
 
     def swap(block, axis, size, low):
-        route = [(i, i + 1) for i in range(low, size - 1, 2)]
+        route = [(i, (i + 1) % size) for i in range(low, size, 2)]
         return lax.ppermute(block, axis, route + [(j, i) for i, j in route])
 
     halo = [

time: 40.1 us -> 36.7 us (0.915); the launches traced: 39.9 us -> 36.1 us
  blocking collectives: 24.4 us -> 17.2 us
  starting transfers between devices: 7.45 us -> 11.2 us
  waiting for transfers between devices: 0.57 us -> 0.12 us
    all_to_all x1, blocking collectives: 24.4 us -> 17.2 us  [per_device(): lax.all_to_all(merged.reshape(slabs // 2, unit, LANES), 'slab', 0, 0, axi...]
    ppermute x4, starting transfers between devices: 5.6 us -> 11.1 us  [swap(): return lax.ppermute(block, axis, route + [(j, i) for i, j in route])]
    ppermute x1, starting transfers between devices: 1.84 us -> 0.09 us  [per_device(): got = lax.ppermute(sent, 'slab', [(i, i ^ 1) for i in range(slabs)])]
    ppermute x4, waiting for transfers between devices: 0.57 us -> 0.01 us  [swap(): return lax.ppermute(block, axis, route + [(j, i) for i, j in route])]
  transfers between devices with their start and end apart: 5 -> 5, of which waited for: 1 -> 1; matrix products, arithmetic and copies ran while one was open for 0% -> 0% of each run, Pallas kernels for 10% -> 11%
where the time goes in v5:
time: 36.7 us; the launch traced here: 36.1 us
  blocking collectives  17.2 us (47%)
  starting transfers between devices  11.2 us (31%)
  Pallas kernels  7.48 us (20%)
    all_to_all x1, blocking collectives, per_device(): lax.all_to_all(merged.reshape(slabs // 2, unit, LANES), 'slab', 0, 0, axi...  17.2 us
    ppermute x4, starting transfers between devices, swap(): return lax.ppermute(block, axis, route + [(j, i) for i, j in route])  11.1 us
    pallas_call x1, Pallas kernels, per_device(): pl.pallas_call(inner_kernel, out_shape=array(ROWS, 4, ROWS, columns), in_...  2.64 us
    pallas_call x1, Pallas kernels, per_device(): pl.pallas_call(lambda *refs: load_kernel(planes * slabs, *refs), out_shap...  1.68 us
    pallas_call x1, Pallas kernels, per_device(): pl.pallas_call(finish_kept, out_shape=half, in_specs=[vmem] * 4, out_spec...  1.41 us
    pallas_call x1, Pallas kernels, per_device(): pl.pallas_call(finish_sent, out_shape=[array(*pad.shape), half], in_specs...  0.92 us
  transfers between devices with their start and end apart: 5, of which 1 were waited for; matrix products, arithmetic and copies ran while one was open for 0% of the time, Pallas kernels for 11%

profile of v5, /device:TPU:8, one launch (start us, length us, event | category | flops | bytes accessed | tf_op | source)
XLA Modules:
  0.0 36.1 jit_solution(3441529004960842674)
XLA Ops:
  0.0 1.7 %load.1 = (f32[18,320,128]{2,1,0:T(8,128)S(1)}, f32[1,64,512]{2,1,0:T(8,128)S(1)}, f32[1,64,512]{2,1,0:T(8,128)S(1)}, f32[16,4,128]{2,1,0:T(4,128)S(1)}, f32[16,...) custom-call(f32[16,64,512]{2,1,0:T(8,128)} %refs_0_.1, s32[8]{0:T(128)} %refs_1_.1, ...), custom_call_target="tpu_custom_call" | custom-call | tf_op jit(solution)/shard_map/load/pallas_call | solution.py:301
  1.7 0.1 collective-permute-start
  1.8 8.2 %collective-permute-start.1 = (f32[1,64,512]{2,1,0:T(8,128)S(1)}, f32[1,64,512]{2,1,0:T(8,128)S(1)}, u32[]{:S(2)}, u32[]{:S(2)}) collective-permute-start(f32[1,64,512]{2,1,0:T(8,128)S(1)} %get-tuple-element.16), channel_id=1, source_target_pairs={{4,8},{12,16},{20,24},{28,32},{36,40},{44,48},{52,56},{60,64},{68,... | collective-permute-start | bytes 393224 | tf_op jit(solution)/shard_map/ppermute | solution.py:323
  9.9 0.4 %collective-permute-start.2 = (f32[16,4,128]{2,1,0:T(4,128)S(1)}, f32[16,4,128]{2,1,0:T(4,128)S(1)}, u32[]{:S(2)}, u32[]{:S(2)}) collective-permute-start(f32[16,4,128]{2,1,0:T(4,128)S(1)} %get-tuple-element.17), channel_id=1, source_target_pairs={{0,1},{2,3},{1,0},{3,2},{4,5},{6,7},{5,4},{7,6},{8,9},{10,11},{9,8... | collective-permute-start | bytes 98312 | tf_op jit(solution)/shard_map/ppermute | solution.py:323
  10.4 2.4 %collective-permute-start.3 = (f32[16,4,128]{2,1,0:T(4,128)S(1)}, f32[16,4,128]{2,1,0:T(4,128)S(1)}, u32[]{:S(2)}, u32[]{:S(2)}) collective-permute-start(f32[16,4,128]{2,1,0:T(4,128)S(1)} %get-tuple-element.18), channel_id=1, source_target_pairs={{1,2},{3,0},{2,1},{0,3},{5,6},{7,4},{6,5},{4,7},{9,10},{11,8},{10,... | collective-permute-start | bytes 98312 | tf_op jit(solution)/shard_map/ppermute | solution.py:323
  12.8 2.6 %inner.1.states = f32[8,4,8,512]{3,2,1,0:T(8,128)S(1)} custom-call(f32[18,320,128]{2,1,0:T(8,128)S(1)} %get-tuple-element.14.pad.pad_in, f32[9,8,128]{2,1,0:T(8,128)S(1)} %get-tuple-element.19.tables_ref.tables, s32[1,512]{1,0:T(1,128)S(1)} %get-tuple-element.20.side_ref.side), custom_call_target="tpu_custom_call" | custom-call | flops 28672000 | bytes 4587520 | tf_op jit(solution)/shard_map/inner/pallas_call | solution.py:339
  15.4 0.0 collective-permute-done.2.row_near
  15.5 0.0 collective-permute-done.3.row_far
  15.5 0.0 collective-permute-done.near
  15.5 0.0 collective-permute-done.1.far
  15.5 0.9 %finish_sent.1 = (f32[18,320,128]{2,1,0:T(8,128)S(1)}, f32[4,4,8,512]{3,2,1,0:T(8,128)S(1)}) custom-call(f32[18,320,128]{2,1,0:T(8,128)S(1)} %get-tuple-element.14.pad.pad_in, f32[1,64,512]{2,1,0:T(8,128)S(1)} %collective-permute-done.near, f32[1,64,512]{2,1,0:T(8,128)S(1)} %collective-permute-done.1.far, ...), custom_call_target="tpu_custom_call", output_to_operand_aliasing={{0}: (0, {})} | custom-call | flops 11878400 | bytes 1900544 | tf_op jit(solution)/shard_map/finish_sent/pallas_call | solution.py:360
  16.4 0.1 collective-permute-start.4
  16.5 1.4 %finish_kept.1.mine = f32[4,4,8,512]{3,2,1,0:T(8,128)S(1)} custom-call(f32[18,320,128]{2,1,0:T(8,128)S(1)} %get-tuple-element.21.pad, f32[8,4,8,512]{3,2,1,0:T(8,128)S(1)} %inner.1.states, f32[9,8,128]{2,1,0:T(8,128)S(1)} %get-tuple-element.19.tables_ref.tables, s32[1,512]{1,0:T(1,128)S(1)} %get-tuple-element.20.side_ref.side), custom_call_target="tpu_custom_call" | custom-call | flops 11878400 | bytes 1900544 | tf_op jit(solution)/shard_map/finish_kept/pallas_call | solution.py:372
  17.9 0.1 collective-permute-done.4.other
  18.0 0.2 pair.1
  18.2 17.2 %all_to_all.5.parts = f32[32,16,128]{2,1,0:T(8,128)S(1)} all-to-all(f32[32,16,128]{2,1,0:T(8,128)S(1)} %bitcast.4), channel_id=1, replica_groups={{0,8,16,24,32,40,48,56,64,72,80,88,96,104,112,120,128,136,144,152,160,1..., dimensions={0} | all-to-all | bytes 524288 | tf_op jit(solution)/shard_map/all_to_all | solution.py:402
  35.4 0.7 %final.1 = f32[16,128]{1,0:T(8,128)} custom-call(f32[32,16,128]{2,1,0:T(8,128)S(1)} %all_to_all.5.parts, s32[4,128]{1,0:T(4,128)S(1)} %bitcast.5), custom_call_target="tpu_custom_call" | custom-call | tf_op jit(solution)/shard_map/final/pallas_call | solution.py:405
Async XLA Ops:
  1.7 13.8 %collective-permute-start = (f32[1,64,512]{2,1,0:T(8,128)S(1)}, f32[1,64,512]{2,1,0:T(8,128)S(1)}, u32[]{:S(2)}, u32[]{:S(2)}) collective-permute-start(f32[1,64,512]{2,1,0:T(8,128)S(1)} %get-tuple-element.15), channel_id=1, source_target_pairs={{0,4},{8,12},{16,20},{24,28},{32,36},{40,44},{48,52},{56,60},{64,6... | collective-permute-start | bytes 393224 | tf_op jit(solution)/shard_map/ppermute | solution.py:323
  1.8 13.7 %collective-permute-start.1 = (f32[1,64,512]{2,1,0:T(8,128)S(1)}, f32[1,64,512]{2,1,0:T(8,128)S(1)}, u32[]{:S(2)}, u32[]{:S(2)}) collective-permute-start(f32[1,64,512]{2,1,0:T(8,128)S(1)} %get-tuple-element.16), channel_id=1, source_target_pairs={{4,8},{12,16},{20,24},{28,32},{36,40},{44,48},{52,56},{60,64},{68,... | collective-permute-start | bytes 393224 | tf_op jit(solution)/shard_map/ppermute | solution.py:323
  9.9 5.5 %collective-permute-start.2 = (f32[16,4,128]{2,1,0:T(4,128)S(1)}, f32[16,4,128]{2,1,0:T(4,128)S(1)}, u32[]{:S(2)}, u32[]{:S(2)}) collective-permute-start(f32[16,4,128]{2,1,0:T(4,128)S(1)} %get-tuple-element.17), channel_id=1, source_target_pairs={{0,1},{2,3},{1,0},{3,2},{4,5},{6,7},{5,4},{7,6},{8,9},{10,11},{9,8... | collective-permute-start | bytes 98312 | tf_op jit(solution)/shard_map/ppermute | solution.py:323
  10.4 5.1 %collective-permute-start.3 = (f32[16,4,128]{2,1,0:T(4,128)S(1)}, f32[16,4,128]{2,1,0:T(4,128)S(1)}, u32[]{:S(2)}, u32[]{:S(2)}) collective-permute-start(f32[16,4,128]{2,1,0:T(4,128)S(1)} %get-tuple-element.18), channel_id=1, source_target_pairs={{1,2},{3,0},{2,1},{0,3},{5,6},{7,4},{6,5},{4,7},{9,10},{11,8},{10,... | collective-permute-start | bytes 98312 | tf_op jit(solution)/shard_map/ppermute | solution.py:323
  16.4 1.6 %collective-permute-start.4 = (f32[4,4,8,512]{3,2,1,0:T(8,128)S(1)}, f32[4,4,8,512]{3,2,1,0:T(8,128)S(1)}, u32[]{:S(2)}, u32[]{:S(2)}) collective-permute-start(f32[4,4,8,512]{3,2,1,0:T(8,128)S(1)} %get-tuple-element.22), channel_id=1, source_target_pairs={{0,4},{4,0},{8,12},{12,8},{16,20},{20,16},{24,28},{28,24},{32,36},... | collective-permute-start | bytes 786440 | tf_op jit(solution)/shard_map/ppermute | solution.py:371

commit v6 on v5

--- a/solution.py
+++ b/solution.py
@@ -318,15 +318,24 @@
         name="load",
     )(*inputs)
 
-    def swap(block, axis, size, low):
-        route = [(i, (i + 1) % size) for i in range(low, size, 2)]
-        return lax.ppermute(block, axis, route + [(j, i) for i, j in route])
+    def swap(block, axis, low):
+        route = []
+        for slab in range(slabs):
+            for tile in range(tiles):
+                index, size = (slab, slabs) if axis == "slab" else (tile, tiles)
+                step = 1 if (index - low) % 2 == 0 else -1
+                if not 0 <= index + step < size:
+                    other = (slab, tile ^ 1) if axis == "slab" else (slab ^ 1, tile)
+                else:
+                    other = (slab + step, tile) if axis == "slab" else (slab, tile + step)
+                route.append((slab * tiles + tile, other[0] * tiles + other[1]))
+        return lax.ppermute(block, ("slab", "tile"), route)
 
     halo = [
-        swap(edges[0], "slab", slabs, 0),
-        swap(edges[1], "slab", slabs, 1),
-        swap(edges[2], "tile", tiles, 0),
-        swap(edges[3], "tile", tiles, 1),
+        swap(edges[0], "slab", 0),
+        swap(edges[1], "slab", 1),
+        swap(edges[2], "tile", 0),
+        swap(edges[3], "tile", 1),
     ]
 
     def cost(steps):

time: 36.7 us -> 36.2 us (0.986); the launches traced: 36.1 us -> 36.1 us
  blocking collectives: 17.2 us -> 24.4 us
  starting transfers between devices: 11.2 us -> 4.17 us
    ppermute x4, starting transfers between devices: 11.1 us -> 3.78 us  [swap(): return lax.ppermute(block, ('slab', 'tile'), route)]
    all_to_all x1, blocking collectives: 17.2 us -> 24.4 us  [per_device(): lax.all_to_all(merged.reshape(slabs // 2, unit, LANES), 'slab', 0, 0, axi...]
  transfers between devices with their start and end apart: 5 -> 5, of which waited for: 1 -> 0; matrix products, arithmetic and copies ran while one was open for 0% -> 0% of each run, Pallas kernels for 11% -> 11%
where the time goes in v6:
time: 36.2 us; the launch traced here: 36.1 us
  blocking collectives  24.4 us (67%)
  Pallas kernels  7.47 us (21%)
  starting transfers between devices  4.17 us (12%)
    all_to_all x1, blocking collectives, per_device(): lax.all_to_all(merged.reshape(slabs // 2, unit, LANES), 'slab', 0, 0, axi...  24.4 us
    ppermute x4, starting transfers between devices, swap(): return lax.ppermute(block, ('slab', 'tile'), route)  3.78 us
    pallas_call x1, Pallas kernels, per_device(): pl.pallas_call(inner_kernel, out_shape=array(ROWS, 4, ROWS, columns), in_...  2.64 us
    pallas_call x1, Pallas kernels, per_device(): pl.pallas_call(lambda *refs: load_kernel(planes * slabs, *refs), out_shap...  1.68 us
    pallas_call x1, Pallas kernels, per_device(): pl.pallas_call(finish_kept, out_shape=half, in_specs=[vmem] * 4, out_spec...  1.4 us
    pallas_call x1, Pallas kernels, per_device(): pl.pallas_call(finish_sent, out_shape=[array(*pad.shape), half], in_specs...  0.92 us
  transfers between devices with their start and end apart: 5, of which 0 were waited for; matrix products, arithmetic and copies ran while one was open for 0% of the time, Pallas kernels for 11%

profile of v6, /device:TPU:8, one launch (start us, length us, event | category | flops | bytes accessed | tf_op | source)
XLA Modules:
  0.0 36.1 jit_solution(7452898721772189001)
XLA Ops:
  0.0 1.7 %load.1 = (f32[18,320,128]{2,1,0:T(8,128)S(1)}, f32[1,64,512]{2,1,0:T(8,128)S(1)}, f32[1,64,512]{2,1,0:T(8,128)S(1)}, f32[16,4,128]{2,1,0:T(4,128)S(1)}, f32[16,...) custom-call(f32[16,64,512]{2,1,0:T(8,128)} %refs_0_.1, s32[8]{0:T(128)} %refs_1_.1, ...), custom_call_target="tpu_custom_call" | custom-call | tf_op jit(solution)/shard_map/load/pallas_call | solution.py:301
  1.7 0.1 collective-permute-start
  1.8 2.3 %collective-permute-start.1 = (f32[1,64,512]{2,1,0:T(8,128)S(1)}, f32[1,64,512]{2,1,0:T(8,128)S(1)}, u32[]{:S(2)}, u32[]{:S(2)}) collective-permute-start(f32[1,64,512]{2,1,0:T(8,128)S(1)} %get-tuple-element.16), channel_id=1, source_target_pairs={{0,1},{1,0},{2,3},{3,2},{4,8},{5,9},{6,10},{7,11},{8,4},{9,5},{10,... | collective-permute-start | bytes 393224 | tf_op jit(solution)/shard_map/ppermute | solution.py:332
  4.1 0.1 collective-permute-start.2
  4.2 1.3 %collective-permute-start.3 = (f32[16,4,128]{2,1,0:T(4,128)S(1)}, f32[16,4,128]{2,1,0:T(4,128)S(1)}, u32[]{:S(2)}, u32[]{:S(2)}) collective-permute-start(f32[16,4,128]{2,1,0:T(4,128)S(1)} %get-tuple-element.18), channel_id=1, source_target_pairs={{0,4},{1,2},{2,1},{3,7},{4,0},{5,6},{6,5},{7,3},{8,12},{9,10},{10,... | collective-permute-start | bytes 98312 | tf_op jit(solution)/shard_map/ppermute | solution.py:332
  5.5 2.6 %inner.1.states = f32[8,4,8,512]{3,2,1,0:T(8,128)S(1)} custom-call(f32[18,320,128]{2,1,0:T(8,128)S(1)} %get-tuple-element.14.pad.pad_in, f32[9,8,128]{2,1,0:T(8,128)S(1)} %get-tuple-element.19.tables_ref.tables, s32[1,512]{1,0:T(1,128)S(1)} %get-tuple-element.20.side_ref.side), custom_call_target="tpu_custom_call" | custom-call | flops 28672000 | bytes 4587520 | tf_op jit(solution)/shard_map/inner/pallas_call | solution.py:348
  8.1 0.0 collective-permute-done.2.row_near
  8.1 0.0 collective-permute-done.3.row_far
  8.1 0.0 collective-permute-done.near
  8.2 0.0 collective-permute-done.1.far
  8.2 0.9 %finish_sent.1 = (f32[18,320,128]{2,1,0:T(8,128)S(1)}, f32[4,4,8,512]{3,2,1,0:T(8,128)S(1)}) custom-call(f32[18,320,128]{2,1,0:T(8,128)S(1)} %get-tuple-element.14.pad.pad_in, f32[1,64,512]{2,1,0:T(8,128)S(1)} %collective-permute-done.near, f32[1,64,512]{2,1,0:T(8,128)S(1)} %collective-permute-done.1.far, ...), custom_call_target="tpu_custom_call", output_to_operand_aliasing={{0}: (0, {})} | custom-call | flops 11878400 | bytes 1900544 | tf_op jit(solution)/shard_map/finish_sent/pallas_call | solution.py:369
  9.1 0.4 %collective-permute-start.4 = (f32[4,4,8,512]{3,2,1,0:T(8,128)S(1)}, f32[4,4,8,512]{3,2,1,0:T(8,128)S(1)}, u32[]{:S(2)}, u32[]{:S(2)}) collective-permute-start(f32[4,4,8,512]{3,2,1,0:T(8,128)S(1)} %get-tuple-element.22), channel_id=1, source_target_pairs={{0,4},{4,0},{8,12},{12,8},{16,20},{20,16},{24,28},{28,24},{32,36},... | collective-permute-start | bytes 786440 | tf_op jit(solution)/shard_map/ppermute | solution.py:380
  9.5 1.4 %finish_kept.1.mine = f32[4,4,8,512]{3,2,1,0:T(8,128)S(1)} custom-call(f32[18,320,128]{2,1,0:T(8,128)S(1)} %get-tuple-element.21.pad, f32[8,4,8,512]{3,2,1,0:T(8,128)S(1)} %inner.1.states, f32[9,8,128]{2,1,0:T(8,128)S(1)} %get-tuple-element.19.tables_ref.tables, s32[1,512]{1,0:T(1,128)S(1)} %get-tuple-element.20.side_ref.side), custom_call_target="tpu_custom_call" | custom-call | flops 11878400 | bytes 1900544 | tf_op jit(solution)/shard_map/finish_kept/pallas_call | solution.py:381
  10.9 0.0 collective-permute-done.4.other
  10.9 0.2 pair.1
  11.1 24.4 %all_to_all.5.parts = f32[32,16,128]{2,1,0:T(8,128)S(1)} all-to-all(f32[32,16,128]{2,1,0:T(8,128)S(1)} %bitcast.4), channel_id=1, replica_groups={{0,8,16,24,32,40,48,56,64,72,80,88,96,104,112,120,128,136,144,152,160,1..., dimensions={0} | all-to-all | bytes 524288 | tf_op jit(solution)/shard_map/all_to_all | solution.py:411
  35.4 0.7 %final.1 = f32[16,128]{1,0:T(8,128)} custom-call(f32[32,16,128]{2,1,0:T(8,128)S(1)} %all_to_all.5.parts, s32[4,128]{1,0:T(4,128)S(1)} %bitcast.5), custom_call_target="tpu_custom_call" | custom-call | tf_op jit(solution)/shard_map/final/pallas_call | solution.py:414
Async XLA Ops:
  1.7 6.5 %collective-permute-start = (f32[1,64,512]{2,1,0:T(8,128)S(1)}, f32[1,64,512]{2,1,0:T(8,128)S(1)}, u32[]{:S(2)}, u32[]{:S(2)}) collective-permute-start(f32[1,64,512]{2,1,0:T(8,128)S(1)} %get-tuple-element.15), channel_id=1, source_target_pairs={{0,4},{1,5},{2,6},{3,7},{4,0},{5,1},{6,2},{7,3},{8,12},{9,13},{10,... | collective-permute-start | bytes 393224 | tf_op jit(solution)/shard_map/ppermute | solution.py:332
  1.8 6.4 %collective-permute-start.1 = (f32[1,64,512]{2,1,0:T(8,128)S(1)}, f32[1,64,512]{2,1,0:T(8,128)S(1)}, u32[]{:S(2)}, u32[]{:S(2)}) collective-permute-start(f32[1,64,512]{2,1,0:T(8,128)S(1)} %get-tuple-element.16), channel_id=1, source_target_pairs={{0,1},{1,0},{2,3},{3,2},{4,8},{5,9},{6,10},{7,11},{8,4},{9,5},{10,... | collective-permute-start | bytes 393224 | tf_op jit(solution)/shard_map/ppermute | solution.py:332
  4.1 4.1 %collective-permute-start.2 = (f32[16,4,128]{2,1,0:T(4,128)S(1)}, f32[16,4,128]{2,1,0:T(4,128)S(1)}, u32[]{:S(2)}, u32[]{:S(2)}) collective-permute-start(f32[16,4,128]{2,1,0:T(4,128)S(1)} %get-tuple-element.17), channel_id=1, source_target_pairs={{0,1},{1,0},{2,3},{3,2},{4,5},{5,4},{6,7},{7,6},{8,9},{9,8},{10,11... | collective-permute-start | bytes 98312 | tf_op jit(solution)/shard_map/ppermute | solution.py:332
  4.2 4.0 %collective-permute-start.3 = (f32[16,4,128]{2,1,0:T(4,128)S(1)}, f32[16,4,128]{2,1,0:T(4,128)S(1)}, u32[]{:S(2)}, u32[]{:S(2)}) collective-permute-start(f32[16,4,128]{2,1,0:T(4,128)S(1)} %get-tuple-element.18), channel_id=1, source_target_pairs={{0,4},{1,2},{2,1},{3,7},{4,0},{5,6},{6,5},{7,3},{8,12},{9,10},{10,... | collective-permute-start | bytes 98312 | tf_op jit(solution)/shard_map/ppermute | solution.py:332
  9.1 1.8 %collective-permute-start.4 = (f32[4,4,8,512]{3,2,1,0:T(8,128)S(1)}, f32[4,4,8,512]{3,2,1,0:T(8,128)S(1)}, u32[]{:S(2)}, u32[]{:S(2)}) collective-permute-start(f32[4,4,8,512]{3,2,1,0:T(8,128)S(1)} %get-tuple-element.22), channel_id=1, source_target_pairs={{0,4},{4,0},{8,12},{12,8},{16,20},{20,16},{24,28},{28,24},{32,36},... | collective-permute-start | bytes 786440 | tf_op jit(solution)/shard_map/ppermute | solution.py:380

commit v7 on v6

--- a/solution.py
+++ b/solution.py
@@ -262,9 +262,10 @@
 
 
 def final_kernel(parts, side_ref, out):
+    ray_order = [k + z for z in range(ROWS) for k in range(0, parts.shape[0], ROWS)]
     toward = jnp.concatenate([side_ref[...]] * 2, axis=0) == 1
     lower = lax.broadcasted_iota(jnp.int32, (ROWS, LANES), 0) < 4
-    whole = [(parts[k, :ROWS], parts[k, ROWS:], both_halves(parts[k, ROWS:])) for k in range(parts.shape[0])]
+    whole = [(parts[k, :ROWS], parts[k, ROWS:], both_halves(parts[k, ROWS:])) for k in ray_order]
     while len(whole) > 1:
         joined = []
         for (top, bottom, passing), (top_2, bottom_2, passing_2) in zip(whole[::2], whole[1::2]):
@@ -397,7 +398,7 @@
             for x in range(groups):
                 whole = merge(front, [mine[x, k, :, c] for k in range(4)], [other[x, k, :, c] for k in range(4)])
                 for k, value in enumerate(whole):
-                    out[pl.ds(x * unit + k * pieces + p, ROWS, stride=groups * unit), :] = value
+                    out[pl.ds(x * ROWS * unit + k * pieces + p, ROWS, stride=unit), :] = value
 
     merged = pl.pallas_call(
         pair,
@@ -407,7 +408,7 @@
         compiler_params=small,
         name="pair",
     )(kept, got, side)
-    members = [[2 * q + c for q in range(slabs // 2)] for c in range(2)]
+    members = [[2 * (z * groups + x) + c for x in range(groups) for z in range(ROWS)] for c in range(2)]
     parts = lax.all_to_all(
         merged.reshape(slabs // 2, unit, LANES), "slab", 0, 0, axis_index_groups=members, tiled=True
     )

time: 36.2 us -> 35.7 us (0.986)
  blocking collectives: 24.4 us -> 23.9 us
    all_to_all x1, blocking collectives: 24.4 us -> 23.9 us  [per_device(): lax.all_to_all(merged.reshape(slabs // 2, unit, LANES), 'slab', 0, 0, axi...]
where the time goes in v7:
time: 35.7 us; the launch traced here: 35.5 us
  blocking collectives  23.9 us (67%)
  Pallas kernels  7.4 us (21%)
  starting transfers between devices  4.17 us (12%)
    all_to_all x1, blocking collectives, per_device(): lax.all_to_all(merged.reshape(slabs // 2, unit, LANES), 'slab', 0, 0, axi...  23.9 us
    ppermute x4, starting transfers between devices, swap(): return lax.ppermute(block, ('slab', 'tile'), route)  3.78 us
    pallas_call x1, Pallas kernels, per_device(): pl.pallas_call(inner_kernel, out_shape=array(ROWS, 4, ROWS, columns), in_...  2.64 us
    pallas_call x1, Pallas kernels, per_device(): pl.pallas_call(lambda *refs: load_kernel(planes * slabs, *refs), out_shap...  1.68 us
    pallas_call x1, Pallas kernels, per_device(): pl.pallas_call(finish_kept, out_shape=half, in_specs=[vmem] * 4, out_spec...  1.4 us
    pallas_call x1, Pallas kernels, per_device(): pl.pallas_call(finish_sent, out_shape=[array(*pad.shape), half], in_specs...  0.92 us
  transfers between devices with their start and end apart: 5, of which 0 were waited for; matrix products, arithmetic and copies ran while one was open for 0% of the time, Pallas kernels for 11%

profile of v7, /device:TPU:8, one launch (start us, length us, event | category | flops | bytes accessed | tf_op | source)
XLA Modules:
  0.0 35.5 jit_solution(6334322785799957681)
XLA Ops:
  0.0 1.7 %load.1 = (f32[18,320,128]{2,1,0:T(8,128)S(1)}, f32[1,64,512]{2,1,0:T(8,128)S(1)}, f32[1,64,512]{2,1,0:T(8,128)S(1)}, f32[16,4,128]{2,1,0:T(4,128)S(1)}, f32[16,...) custom-call(f32[16,64,512]{2,1,0:T(8,128)} %refs_0_.1, s32[8]{0:T(128)} %refs_1_.1, ...), custom_call_target="tpu_custom_call" | custom-call | tf_op jit(solution)/shard_map/load/pallas_call | solution.py:302
  1.7 0.1 collective-permute-start
  1.8 2.3 %collective-permute-start.1 = (f32[1,64,512]{2,1,0:T(8,128)S(1)}, f32[1,64,512]{2,1,0:T(8,128)S(1)}, u32[]{:S(2)}, u32[]{:S(2)}) collective-permute-start(f32[1,64,512]{2,1,0:T(8,128)S(1)} %get-tuple-element.16), channel_id=1, source_target_pairs={{0,1},{1,0},{2,3},{3,2},{4,8},{5,9},{6,10},{7,11},{8,4},{9,5},{10,... | collective-permute-start | bytes 393224 | tf_op jit(solution)/shard_map/ppermute | solution.py:333
  4.1 0.1 collective-permute-start.2
  4.2 1.3 %collective-permute-start.3 = (f32[16,4,128]{2,1,0:T(4,128)S(1)}, f32[16,4,128]{2,1,0:T(4,128)S(1)}, u32[]{:S(2)}, u32[]{:S(2)}) collective-permute-start(f32[16,4,128]{2,1,0:T(4,128)S(1)} %get-tuple-element.18), channel_id=1, source_target_pairs={{0,4},{1,2},{2,1},{3,7},{4,0},{5,6},{6,5},{7,3},{8,12},{9,10},{10,... | collective-permute-start | bytes 98312 | tf_op jit(solution)/shard_map/ppermute | solution.py:333
  5.5 2.6 %inner.1.states = f32[8,4,8,512]{3,2,1,0:T(8,128)S(1)} custom-call(f32[18,320,128]{2,1,0:T(8,128)S(1)} %get-tuple-element.14.pad.pad_in, f32[9,8,128]{2,1,0:T(8,128)S(1)} %get-tuple-element.19.tables_ref.tables, s32[1,512]{1,0:T(1,128)S(1)} %get-tuple-element.20.side_ref.side), custom_call_target="tpu_custom_call" | custom-call | flops 28672000 | bytes 4587520 | tf_op jit(solution)/shard_map/inner/pallas_call | solution.py:349
  8.1 0.0 collective-permute-done.2.row_near
  8.1 0.0 collective-permute-done.3.row_far
  8.1 0.0 collective-permute-done.near
  8.2 0.0 collective-permute-done.1.far
  8.2 0.9 %finish_sent.1 = (f32[18,320,128]{2,1,0:T(8,128)S(1)}, f32[4,4,8,512]{3,2,1,0:T(8,128)S(1)}) custom-call(f32[18,320,128]{2,1,0:T(8,128)S(1)} %get-tuple-element.14.pad.pad_in, f32[1,64,512]{2,1,0:T(8,128)S(1)} %collective-permute-done.near, f32[1,64,512]{2,1,0:T(8,128)S(1)} %collective-permute-done.1.far, ...), custom_call_target="tpu_custom_call", output_to_operand_aliasing={{0}: (0, {})} | custom-call | flops 11878400 | bytes 1900544 | tf_op jit(solution)/shard_map/finish_sent/pallas_call | solution.py:370
  9.1 0.4 %collective-permute-start.4 = (f32[4,4,8,512]{3,2,1,0:T(8,128)S(1)}, f32[4,4,8,512]{3,2,1,0:T(8,128)S(1)}, u32[]{:S(2)}, u32[]{:S(2)}) collective-permute-start(f32[4,4,8,512]{3,2,1,0:T(8,128)S(1)} %get-tuple-element.22), channel_id=1, source_target_pairs={{0,4},{4,0},{8,12},{12,8},{16,20},{20,16},{24,28},{28,24},{32,36},... | collective-permute-start | bytes 786440 | tf_op jit(solution)/shard_map/ppermute | solution.py:381
  9.5 1.4 %finish_kept.1.mine = f32[4,4,8,512]{3,2,1,0:T(8,128)S(1)} custom-call(f32[18,320,128]{2,1,0:T(8,128)S(1)} %get-tuple-element.21.pad, f32[8,4,8,512]{3,2,1,0:T(8,128)S(1)} %inner.1.states, f32[9,8,128]{2,1,0:T(8,128)S(1)} %get-tuple-element.19.tables_ref.tables, s32[1,512]{1,0:T(1,128)S(1)} %get-tuple-element.20.side_ref.side), custom_call_target="tpu_custom_call" | custom-call | flops 11878400 | bytes 1900544 | tf_op jit(solution)/shard_map/finish_kept/pallas_call | solution.py:382
  10.9 0.0 collective-permute-done.4.other
  10.9 0.1 pair.1
  11.0 23.9 %all_to_all.5.parts = f32[32,16,128]{2,1,0:T(8,128)S(1)} all-to-all(f32[32,16,128]{2,1,0:T(8,128)S(1)} %bitcast.4), channel_id=1, replica_groups={{0,32,64,96,128,160,192,224,8,40,72,104,136,168,200,232,16,48,80,112,14..., dimensions={0} | all-to-all | bytes 524288 | tf_op jit(solution)/shard_map/all_to_all | solution.py:412
  34.9 0.7 %final.1 = f32[16,128]{1,0:T(8,128)} custom-call(f32[32,16,128]{2,1,0:T(8,128)S(1)} %all_to_all.5.parts, s32[4,128]{1,0:T(4,128)S(1)} %bitcast.5), custom_call_target="tpu_custom_call" | custom-call | tf_op jit(solution)/shard_map/final/pallas_call | solution.py:415
Async XLA Ops:
  1.7 6.5 %collective-permute-start = (f32[1,64,512]{2,1,0:T(8,128)S(1)}, f32[1,64,512]{2,1,0:T(8,128)S(1)}, u32[]{:S(2)}, u32[]{:S(2)}) collective-permute-start(f32[1,64,512]{2,1,0:T(8,128)S(1)} %get-tuple-element.15), channel_id=1, source_target_pairs={{0,4},{1,5},{2,6},{3,7},{4,0},{5,1},{6,2},{7,3},{8,12},{9,13},{10,... | collective-permute-start | bytes 393224 | tf_op jit(solution)/shard_map/ppermute | solution.py:333
  1.8 6.4 %collective-permute-start.1 = (f32[1,64,512]{2,1,0:T(8,128)S(1)}, f32[1,64,512]{2,1,0:T(8,128)S(1)}, u32[]{:S(2)}, u32[]{:S(2)}) collective-permute-start(f32[1,64,512]{2,1,0:T(8,128)S(1)} %get-tuple-element.16), channel_id=1, source_target_pairs={{0,1},{1,0},{2,3},{3,2},{4,8},{5,9},{6,10},{7,11},{8,4},{9,5},{10,... | collective-permute-start | bytes 393224 | tf_op jit(solution)/shard_map/ppermute | solution.py:333
  4.1 4.1 %collective-permute-start.2 = (f32[16,4,128]{2,1,0:T(4,128)S(1)}, f32[16,4,128]{2,1,0:T(4,128)S(1)}, u32[]{:S(2)}, u32[]{:S(2)}) collective-permute-start(f32[16,4,128]{2,1,0:T(4,128)S(1)} %get-tuple-element.17), channel_id=1, source_target_pairs={{0,1},{1,0},{2,3},{3,2},{4,5},{5,4},{6,7},{7,6},{8,9},{9,8},{10,11... | collective-permute-start | bytes 98312 | tf_op jit(solution)/shard_map/ppermute | solution.py:333
  4.2 4.0 %collective-permute-start.3 = (f32[16,4,128]{2,1,0:T(4,128)S(1)}, f32[16,4,128]{2,1,0:T(4,128)S(1)}, u32[]{:S(2)}, u32[]{:S(2)}) collective-permute-start(f32[16,4,128]{2,1,0:T(4,128)S(1)} %get-tuple-element.18), channel_id=1, source_target_pairs={{0,4},{1,2},{2,1},{3,7},{4,0},{5,6},{6,5},{7,3},{8,12},{9,10},{10,... | collective-permute-start | bytes 98312 | tf_op jit(solution)/shard_map/ppermute | solution.py:333
  9.1 1.8 %collective-permute-start.4 = (f32[4,4,8,512]{3,2,1,0:T(8,128)S(1)}, f32[4,4,8,512]{3,2,1,0:T(8,128)S(1)}, u32[]{:S(2)}, u32[]{:S(2)}) collective-permute-start(f32[4,4,8,512]{3,2,1,0:T(8,128)S(1)} %get-tuple-element.22), channel_id=1, source_target_pairs={{0,4},{4,0},{8,12},{12,8},{16,20},{20,16},{24,28},{28,24},{32,36},... | collective-permute-start | bytes 786440 | tf_op jit(solution)/shard_map/ppermute | solution.py:381
